TPU v7x, 32 devices: a whole 2x2x4 slice. The times are simulated.
32 devices in a mesh: section: 8 (over y, x, core), dp: 4 (over z).
Axes of the slice: x: 2, y: 2, z: 4, core: 2. Of those that a mesh axis runs over, the one named last changes fastest.
Arguments:
- latents: bfloat16 [4, 512, 320], P(None, 'dp'), may hold values from -6 to 6
- steps: int32 [4, 4], P('dp'), may hold values from 0 to 999
- cotangent: bfloat16 [4, 512, 320], P(None, 'dp'), may hold values from -0.119628906 to 0.119628906
- w_in: bfloat16 [8, 320, 1280], P('section'), may hold values from -0.3125 to 0.3125
- w_out: bfloat16 [8, 1280, 320], P('section'), may hold values from -0.15625 to 0.15625
- w_time: bfloat16 [8, 320, 1280], P('section'), may hold values from -0.3125 to 0.3125
- w_skip: bfloat16 [8, 320, 320], P('section'), may hold values from -0.3125 to 0.3125
Outputs:
- section_out: bfloat16 [8, 4, 512, 320], P('section', None, 'dp')
- grad_w_in: float32 [8, 320, 1280], P('section')
- grad_w_out: float32 [8, 1280, 320], P('section')
- grad_w_time: float32 [8, 320, 1280], P('section')
- grad_w_skip: float32 [8, 320, 320], P('section')
All inputs are finite; a program needn't handle non-finite values.
Results may differ from a plain program's by a relative error of at most 0.03.
Values may be sent and summed in bfloat16 or wider, within the bound.
No kernel may reach another device: no remote copies, remote signals or barrier semaphores. Data moves between devices by JAX's collectives and lax.ppermute only.
A program may use at most 64 MiB of HBM per device.

v0:
```python
import math

import jax
import jax.numpy as jnp
from jax import lax
from jax.sharding import PartitionSpec as P


def passed_along(block, axis, distance):
    devices = range(lax.axis_size(axis))
    route = [(i - distance, i) for i in devices if i - distance in devices]
    return lax.ppermute(block, axis, route)


def contract_rows(left, right):
    return lax.dot_general(
        left, right, (((0,), (0,)), ((), ())), preferred_element_type=jnp.float32
    )


def contract_cols(left, right):
    return lax.dot_general(
        left, right, (((1,), (1,)), ((), ())), preferred_element_type=jnp.float32
    )


def gelu_tanh(values):
    return jax.nn.gelu(values, approximate=True)


def embed(step_value, width):
    half_width = width // 2
    position = jnp.arange(half_width).astype(jnp.float32)
    frequency = jnp.exp(-math.log(10000.0) * position / half_width)
    angle = step_value.astype(jnp.float32) * frequency
    return jnp.concatenate([jnp.sin(angle), jnp.cos(angle)]).astype(jnp.bfloat16)


def inner_block(merged, w_first, w_second, w_clock, clock_code):
    widened = merged.astype(jnp.float32)
    scale = lax.rsqrt(jnp.mean(widened * widened, axis=-1, keepdims=True) + 1e-05)
    normed = (widened * scale).astype(jnp.bfloat16)
    preact = jnp.dot(normed, w_first, preferred_element_type=jnp.float32) + jnp.dot(
        clock_code[None, :], w_clock, preferred_element_type=jnp.float32
    )
    hidden = gelu_tanh(preact).astype(jnp.bfloat16)
    result = (widened + jnp.dot(hidden, w_second, preferred_element_type=jnp.float32)).astype(
        jnp.bfloat16
    )
    return (result, widened, scale, normed, preact, hidden)


def block_forward(arriving, skip_rows, w_first, w_second, w_clock, w_merge, clock_code):
    merged = (
        arriving.astype(jnp.float32)
        + jnp.dot(skip_rows, w_merge, preferred_element_type=jnp.float32)
    ).astype(jnp.bfloat16)
    result = inner_block(merged, w_first, w_second, w_clock, clock_code)[0]
    return (result, merged)


def block_backward(out_grad, merged, skip_rows, w_first, w_second, w_clock, w_merge, clock_code):
    result, widened, scale, normed, preact, hidden = inner_block(
        merged, w_first, w_second, w_clock, clock_code
    )
    grad_second = contract_rows(hidden, out_grad)
    hidden_grad = contract_cols(out_grad, w_second)
    pre_grad = jax.vjp(gelu_tanh, preact)[1](hidden_grad)[0].astype(jnp.bfloat16)
    grad_first = contract_rows(normed, pre_grad)
    grad_clock = (
        clock_code.astype(jnp.float32)[:, None]
        * jnp.sum(pre_grad.astype(jnp.float32), axis=0)[None, :]
    )
    norm_grad = contract_cols(pre_grad, w_first)
    unit = widened * scale
    merged_grad = (
        out_grad.astype(jnp.float32)
        + scale * (norm_grad - unit * jnp.mean(norm_grad * unit, axis=-1, keepdims=True))
    ).astype(jnp.bfloat16)
    grad_merge = contract_rows(skip_rows, merged_grad)
    skip_grad = contract_cols(merged_grad, w_merge).astype(jnp.bfloat16)
    return (merged_grad, skip_grad, (grad_first, grad_second, grad_clock, grad_merge))


def keep(buffer, position, flag, value):
    return buffer.at[position].set(jnp.where(flag, value, buffer[position]))


def local(latents, steps, cotangent, w_in, w_out, w_time, w_skip):
    sections = lax.axis_size("section")
    rank = lax.axis_index("section")
    half = sections // 2
    mirror = sections - 1 - rank
    upper = rank >= half
    w_first = w_in[0]
    w_second = w_out[0]
    w_clock = w_time[0]
    w_merge = w_skip[0]
    micro = latents.shape[0]
    height = latents.shape[1]
    width = latents.shape[2]
    table = jnp.stack([embed(steps[0, which], width) for which in range(micro)])
    ticks = micro + sections - 1
    blank = jnp.zeros((height, width), jnp.bfloat16)
    buffer = jnp.zeros((micro, height, width), jnp.bfloat16)
    stack_blank = jnp.zeros((half, height, width), jnp.bfloat16)
    slot_down = jnp.minimum(rank, half - 1)
    slot_up = jnp.clip(mirror, 0, half - 1)

    def forward(tick, carry):
        incoming, stack, inputs, skips, outputs, received = carry
        batch = tick - rank
        valid = (batch >= 0) & (batch < micro)
        index = jnp.clip(batch, 0, micro - 1)
        arriving = jnp.where(rank == 0, latents[index], incoming)
        skip_rows = jnp.where(upper, stack[slot_up], blank)
        result, merged = block_forward(
            arriving, skip_rows, w_first, w_second, w_clock, w_merge, table[index]
        )
        inputs = keep(inputs, index, valid, merged)
        skips = keep(skips, index, valid, skip_rows)
        outputs = keep(outputs, index, valid, result)
        stack = stack.at[slot_down].set(jnp.where(upper, stack[slot_down], result))
        incoming, stack = passed_along((result, stack), "section", 1)
        return (incoming, stack, inputs, skips, outputs, received)

    start = (blank, stack_blank, buffer, buffer, buffer, buffer)
    incoming, stack, inputs, skips, outputs, received = lax.fori_loop(0, ticks, forward, start)

    def backward(tick, carry):
        incoming, stack, returned, totals = carry
        batch = tick - mirror
        valid = (batch >= 0) & (batch < micro)
        index = jnp.clip(batch, 0, micro - 1)
        arriving = jnp.where(rank == sections - 1, cotangent[index], incoming)
        extra = jnp.where(upper, blank, stack[slot_down])
        out_grad = (arriving.astype(jnp.float32) + extra.astype(jnp.float32)).astype(jnp.bfloat16)
        merged_grad, skip_grad, parts = block_backward(
            out_grad, inputs[index], skips[index], w_first, w_second, w_clock, w_merge, table[index]
        )
        totals = tuple((total + jnp.where(valid, part, 0.0) for total, part in zip(totals, parts)))
        stack = stack.at[slot_up].set(jnp.where(upper, skip_grad, stack[slot_up]))
        incoming, stack = passed_along((merged_grad, stack), "section", -1)
        return (incoming, stack, returned, totals)

    zero_totals = (
        jnp.zeros(w_first.shape, jnp.float32),
        jnp.zeros(w_second.shape, jnp.float32),
        jnp.zeros(w_clock.shape, jnp.float32),
        jnp.zeros(w_merge.shape, jnp.float32),
    )
    incoming, stack, returned, totals = lax.fori_loop(
        0, ticks, backward, (blank, stack_blank, buffer, zero_totals)
    )
    summed = (
        lax.psum(totals[0].astype(jnp.bfloat16), "dp").astype(jnp.float32),
        lax.psum(totals[1].astype(jnp.bfloat16), "dp").astype(jnp.float32),
        lax.psum(totals[2].astype(jnp.bfloat16), "dp").astype(jnp.float32),
        lax.psum(totals[3].astype(jnp.bfloat16), "dp").astype(jnp.float32),
    )
    return (outputs[None], summed[0][None], summed[1][None], summed[2][None], summed[3][None])


def solution(mesh):
    placed = (
        P(None, "dp", None),
        P("dp", None),
        P(None, "dp", None),
        P("section", None, None),
        P("section", None, None),
        P("section", None, None),
        P("section", None, None),
    )
    return jax.shard_map(
        local,
        mesh=mesh,
        in_specs=placed,
        out_specs=(
            P("section", None, "dp", None),
            P("section", None, None),
            P("section", None, None),
            P("section", None, None),
            P("section", None, None),
        ),
        check_vma=False,
    )
```

profile of v0, /device:TPU:4, one launch (start us, length us, event | category | flops | bytes accessed | tf_op | source)
XLA Modules:
  0.0 635.5 jit_solution(18374547293806633850)
XLA Ops:
  17.2 239.9 %while.57 = (s32[]{:T(128)}, bf16[128,320]{0,1:T(8,128)(2,1)S(1)}, bf16[4,128,320]{1,2,0:T(8,128)(2,1)}, bf16[4,128,320]{1,2,0:T(8,128)(2,1)}, bf16[4,128,320]{1...) while((s32[]{:T(128)}, bf16[128,320]{0,1:T(8,128)(2,1)S(1)}, ...), condition=%wide.region_4.5_spmd, body=%wide.region_0.4_spmd.sunk | while | flops 239329440 | bytes 6903196 | solution.py:128
  21.7 4.0 fusion.142
  27.7 3.5 collective-permute-start.1
  33.3 4.0 collective-permute-done.1
  43.5 4.0 fusion.142
  54.2 4.9 collective-permute-done.1
  65.4 4.0 fusion.142
  75.4 5.5 collective-permute-done.1
  87.2 4.0 fusion.142
  97.2 5.5 collective-permute-done.1
  109.0 4.0 fusion.142
  119.9 4.7 collective-permute-done.1
  130.8 4.0 fusion.142
  141.7 4.7 collective-permute-done.1
  152.6 4.0 fusion.142
  163.5 4.7 collective-permute-done.1
  174.4 4.0 fusion.142
  185.3 4.6 collective-permute-done.1
  196.2 4.0 fusion.142
  206.2 5.5 collective-permute-done.1
  218.0 4.0 fusion.142
  228.0 5.5 collective-permute-done.1
  239.8 4.0 fusion.142
  249.8 5.5 collective-permute-done.1
  258.5 246.1 %while.58 = (s32[]{:T(128)}, bf16[128,320]{0,1:T(8,128)(2,1)}, bf16[4,128,320]{1,2,0:T(8,128)(2,1)}, f32[320,1280]{1,0:T(8,128)}, f32[1280,320]{0,1:T(8,128)S(1)...) while((s32[]{:T(128)}, bf16[128,320]{0,1:T(8,128)(2,1)}, ...), condition=%wide.region_10.11_spmd.clone, body=%wide.region_6.10_spmd.clone.sunk | while | flops 588410048 | bytes 43250144 | solution.py:152
  295.8 3.0 fusion.163
  318.3 3.0 fusion.163
  340.7 3.0 fusion.163
  363.1 3.0 fusion.163
  385.6 3.0 fusion.163
  430.4 3.0 fusion.163
  510.7 111.0 %all-reduce.3.cloned.1.call-done = (bf16[1,320,1280]{2,1,0:T(8,128)(2,1)}, bf16[1,1280,320]{1,2,0:T(8,128)(2,1)}, bf16[1,320,1280]{2,1,0:T(8,128)(2,1)}, bf16[1,320,320]{2,1,0:T(8,128)(2,1)}) async-done(((bf16[1,320,1280]{2,1,0:T(8,128)(2,1)}, bf16[1,1280,320]{1,2,0:T(8,128)(2,1)}, bf16[1,320,1280]{2,1,0:T(8,128)(2,1)}, bf16[1,320,320]{2,1,0:T(8,128)(2,1)}), (bf16[1,320,1280]{2,1,0:T(8,128)(2,1)}, ...) | async-done | bytes 2662416 | tf_op jit(solution)/shard_map/psum | solution.py:156
  (546 shorter events, 385.4 us)
Async XLA Ops:
  7.2 614.5 %all-reduce.3.cloned.1.call-start = ((), (), s32[]{:S(2)}) async-start(), calls=%async_computation | async-start | bytes 5406720 | tf_op jit(solution)/shard_map/psum | solution.py:156
  25.7 13.2 %collective-permute-start = (bf16[128,320]{0,1:T(8,128)(2,1)}, bf16[128,320]{0,1:T(8,128)(2,1)S(1)}, u32[]{:S(2)}, u32[]{:S(2)}) collective-permute-start(bf16[128,320]{0,1:T(8,128)(2,1)} %get-tuple-element.1666), channel_id=1, source_target_pairs={{0,4},{4,8},{8,12},{12,16},{16,20},{20,24},{24,28},{1,5},{5,9},{9,... | collective-permute-start | bytes 245768 | tf_op jit(solution)/shard_map/while/body/eval_jaxpr/ppermute | solution.py:12
  47.6 13.2 %collective-permute-start = (bf16[128,320]{0,1:T(8,128)(2,1)}, bf16[128,320]{0,1:T(8,128)(2,1)S(1)}, u32[]{:S(2)}, u32[]{:S(2)}) collective-permute-start(bf16[128,320]{0,1:T(8,128)(2,1)} %get-tuple-element.1666), channel_id=1, source_target_pairs={{0,4},{4,8},{8,12},{12,16},{16,20},{20,24},{24,28},{1,5},{5,9},{9,... | collective-permute-start | bytes 245768 | tf_op jit(solution)/shard_map/while/body/eval_jaxpr/ppermute | solution.py:12
  69.4 13.2 %collective-permute-start = (bf16[128,320]{0,1:T(8,128)(2,1)}, bf16[128,320]{0,1:T(8,128)(2,1)S(1)}, u32[]{:S(2)}, u32[]{:S(2)}) collective-permute-start(bf16[128,320]{0,1:T(8,128)(2,1)} %get-tuple-element.1666), channel_id=1, source_target_pairs={{0,4},{4,8},{8,12},{12,16},{16,20},{20,24},{24,28},{1,5},{5,9},{9,... | collective-permute-start | bytes 245768 | tf_op jit(solution)/shard_map/while/body/eval_jaxpr/ppermute | solution.py:12
  91.2 13.2 %collective-permute-start = (bf16[128,320]{0,1:T(8,128)(2,1)}, bf16[128,320]{0,1:T(8,128)(2,1)S(1)}, u32[]{:S(2)}, u32[]{:S(2)}) collective-permute-start(bf16[128,320]{0,1:T(8,128)(2,1)} %get-tuple-element.1666), channel_id=1, source_target_pairs={{0,4},{4,8},{8,12},{12,16},{16,20},{20,24},{24,28},{1,5},{5,9},{9,... | collective-permute-start | bytes 245768 | tf_op jit(solution)/shard_map/while/body/eval_jaxpr/ppermute | solution.py:12
  113.0 13.2 %collective-permute-start = (bf16[128,320]{0,1:T(8,128)(2,1)}, bf16[128,320]{0,1:T(8,128)(2,1)S(1)}, u32[]{:S(2)}, u32[]{:S(2)}) collective-permute-start(bf16[128,320]{0,1:T(8,128)(2,1)} %get-tuple-element.1666), channel_id=1, source_target_pairs={{0,4},{4,8},{8,12},{12,16},{16,20},{20,24},{24,28},{1,5},{5,9},{9,... | collective-permute-start | bytes 245768 | tf_op jit(solution)/shard_map/while/body/eval_jaxpr/ppermute | solution.py:12
  134.8 13.2 %collective-permute-start = (bf16[128,320]{0,1:T(8,128)(2,1)}, bf16[128,320]{0,1:T(8,128)(2,1)S(1)}, u32[]{:S(2)}, u32[]{:S(2)}) collective-permute-start(bf16[128,320]{0,1:T(8,128)(2,1)} %get-tuple-element.1666), channel_id=1, source_target_pairs={{0,4},{4,8},{8,12},{12,16},{16,20},{20,24},{24,28},{1,5},{5,9},{9,... | collective-permute-start | bytes 245768 | tf_op jit(solution)/shard_map/while/body/eval_jaxpr/ppermute | solution.py:12
  156.6 13.2 %collective-permute-start = (bf16[128,320]{0,1:T(8,128)(2,1)}, bf16[128,320]{0,1:T(8,128)(2,1)S(1)}, u32[]{:S(2)}, u32[]{:S(2)}) collective-permute-start(bf16[128,320]{0,1:T(8,128)(2,1)} %get-tuple-element.1666), channel_id=1, source_target_pairs={{0,4},{4,8},{8,12},{12,16},{16,20},{20,24},{24,28},{1,5},{5,9},{9,... | collective-permute-start | bytes 245768 | tf_op jit(solution)/shard_map/while/body/eval_jaxpr/ppermute | solution.py:12
  178.4 13.2 %collective-permute-start = (bf16[128,320]{0,1:T(8,128)(2,1)}, bf16[128,320]{0,1:T(8,128)(2,1)S(1)}, u32[]{:S(2)}, u32[]{:S(2)}) collective-permute-start(bf16[128,320]{0,1:T(8,128)(2,1)} %get-tuple-element.1666), channel_id=1, source_target_pairs={{0,4},{4,8},{8,12},{12,16},{16,20},{20,24},{24,28},{1,5},{5,9},{9,... | collective-permute-start | bytes 245768 | tf_op jit(solution)/shard_map/while/body/eval_jaxpr/ppermute | solution.py:12
  200.2 13.2 %collective-permute-start = (bf16[128,320]{0,1:T(8,128)(2,1)}, bf16[128,320]{0,1:T(8,128)(2,1)S(1)}, u32[]{:S(2)}, u32[]{:S(2)}) collective-permute-start(bf16[128,320]{0,1:T(8,128)(2,1)} %get-tuple-element.1666), channel_id=1, source_target_pairs={{0,4},{4,8},{8,12},{12,16},{16,20},{20,24},{24,28},{1,5},{5,9},{9,... | collective-permute-start | bytes 245768 | tf_op jit(solution)/shard_map/while/body/eval_jaxpr/ppermute | solution.py:12
  222.0 13.2 %collective-permute-start = (bf16[128,320]{0,1:T(8,128)(2,1)}, bf16[128,320]{0,1:T(8,128)(2,1)S(1)}, u32[]{:S(2)}, u32[]{:S(2)}) collective-permute-start(bf16[128,320]{0,1:T(8,128)(2,1)} %get-tuple-element.1666), channel_id=1, source_target_pairs={{0,4},{4,8},{8,12},{12,16},{16,20},{20,24},{24,28},{1,5},{5,9},{9,... | collective-permute-start | bytes 245768 | tf_op jit(solution)/shard_map/while/body/eval_jaxpr/ppermute | solution.py:12
  243.8 13.2 %collective-permute-start = (bf16[128,320]{0,1:T(8,128)(2,1)}, bf16[128,320]{0,1:T(8,128)(2,1)S(1)}, u32[]{:S(2)}, u32[]{:S(2)}) collective-permute-start(bf16[128,320]{0,1:T(8,128)(2,1)} %get-tuple-element.1666), channel_id=1, source_target_pairs={{0,4},{4,8},{8,12},{12,16},{16,20},{20,24},{24,28},{1,5},{5,9},{9,... | collective-permute-start | bytes 245768 | tf_op jit(solution)/shard_map/while/body/eval_jaxpr/ppermute | solution.py:12
  263.8 16.4 %collective-permute-start.2 = (bf16[128,320]{0,1:T(8,128)(2,1)}, bf16[128,320]{0,1:T(8,128)(2,1)}, u32[]{:S(2)}, u32[]{:S(2)}) collective-permute-start(bf16[128,320]{0,1:T(8,128)(2,1)} %fusion.161), channel_id=1, source_target_pairs={{4,0},{8,4},{12,8},{16,12},{20,16},{24,20},{28,24},{5,1},{9,5},{13... | collective-permute-start | bytes 245768 | tf_op jit(solution)/shard_map/while/body/eval_jaxpr/ppermute | solution.py:12
  285.4 17.3 %collective-permute-start.2 = (bf16[128,320]{0,1:T(8,128)(2,1)}, bf16[128,320]{0,1:T(8,128)(2,1)}, u32[]{:S(2)}, u32[]{:S(2)}) collective-permute-start(bf16[128,320]{0,1:T(8,128)(2,1)} %fusion.161), channel_id=1, source_target_pairs={{4,0},{8,4},{12,8},{16,12},{20,16},{24,20},{28,24},{5,1},{9,5},{13... | collective-permute-start | bytes 245768 | tf_op jit(solution)/shard_map/while/body/eval_jaxpr/ppermute | solution.py:12
  290.8 10.2 %collective-permute-start.3 = (bf16[4,128,320]{1,2,0:T(8,128)(2,1)}, bf16[4,128,320]{1,2,0:T(8,128)(2,1)}, u32[]{:S(2)}, u32[]{:S(2)}) collective-permute-start(bf16[4,128,320]{1,2,0:T(8,128)(2,1)} %fusion.162), channel_id=1, source_target_pairs={{4,0},{8,4},{12,8},{16,12},{20,16},{24,20},{28,24},{5,1},{9,5},{13... | collective-permute-start | bytes 983048 | tf_op jit(solution)/shard_map/while/body/eval_jaxpr/ppermute | solution.py:12
  308.0 17.1 %collective-permute-start.2 = (bf16[128,320]{0,1:T(8,128)(2,1)}, bf16[128,320]{0,1:T(8,128)(2,1)}, u32[]{:S(2)}, u32[]{:S(2)}) collective-permute-start(bf16[128,320]{0,1:T(8,128)(2,1)} %fusion.161), channel_id=1, source_target_pairs={{4,0},{8,4},{12,8},{16,12},{20,16},{24,20},{28,24},{5,1},{9,5},{13... | collective-permute-start | bytes 245768 | tf_op jit(solution)/shard_map/while/body/eval_jaxpr/ppermute | solution.py:12
  313.2 10.2 %collective-permute-start.3 = (bf16[4,128,320]{1,2,0:T(8,128)(2,1)}, bf16[4,128,320]{1,2,0:T(8,128)(2,1)}, u32[]{:S(2)}, u32[]{:S(2)}) collective-permute-start(bf16[4,128,320]{1,2,0:T(8,128)(2,1)} %fusion.162), channel_id=1, source_target_pairs={{4,0},{8,4},{12,8},{16,12},{20,16},{24,20},{28,24},{5,1},{9,5},{13... | collective-permute-start | bytes 983048 | tf_op jit(solution)/shard_map/while/body/eval_jaxpr/ppermute | solution.py:12
  330.4 17.1 %collective-permute-start.2 = (bf16[128,320]{0,1:T(8,128)(2,1)}, bf16[128,320]{0,1:T(8,128)(2,1)}, u32[]{:S(2)}, u32[]{:S(2)}) collective-permute-start(bf16[128,320]{0,1:T(8,128)(2,1)} %fusion.161), channel_id=1, source_target_pairs={{4,0},{8,4},{12,8},{16,12},{20,16},{24,20},{28,24},{5,1},{9,5},{13... | collective-permute-start | bytes 245768 | tf_op jit(solution)/shard_map/while/body/eval_jaxpr/ppermute | solution.py:12
  335.6 10.2 %collective-permute-start.3 = (bf16[4,128,320]{1,2,0:T(8,128)(2,1)}, bf16[4,128,320]{1,2,0:T(8,128)(2,1)}, u32[]{:S(2)}, u32[]{:S(2)}) collective-permute-start(bf16[4,128,320]{1,2,0:T(8,128)(2,1)} %fusion.162), channel_id=1, source_target_pairs={{4,0},{8,4},{12,8},{16,12},{20,16},{24,20},{28,24},{5,1},{9,5},{13... | collective-permute-start | bytes 983048 | tf_op jit(solution)/shard_map/while/body/eval_jaxpr/ppermute | solution.py:12
  352.9 17.1 %collective-permute-start.2 = (bf16[128,320]{0,1:T(8,128)(2,1)}, bf16[128,320]{0,1:T(8,128)(2,1)}, u32[]{:S(2)}, u32[]{:S(2)}) collective-permute-start(bf16[128,320]{0,1:T(8,128)(2,1)} %fusion.161), channel_id=1, source_target_pairs={{4,0},{8,4},{12,8},{16,12},{20,16},{24,20},{28,24},{5,1},{9,5},{13... | collective-permute-start | bytes 245768 | tf_op jit(solution)/shard_map/while/body/eval_jaxpr/ppermute | solution.py:12
  358.1 10.2 %collective-permute-start.3 = (bf16[4,128,320]{1,2,0:T(8,128)(2,1)}, bf16[4,128,320]{1,2,0:T(8,128)(2,1)}, u32[]{:S(2)}, u32[]{:S(2)}) collective-permute-start(bf16[4,128,320]{1,2,0:T(8,128)(2,1)} %fusion.162), channel_id=1, source_target_pairs={{4,0},{8,4},{12,8},{16,12},{20,16},{24,20},{28,24},{5,1},{9,5},{13... | collective-permute-start | bytes 983048 | tf_op jit(solution)/shard_map/while/body/eval_jaxpr/ppermute | solution.py:12
  375.3 17.1 %collective-permute-start.2 = (bf16[128,320]{0,1:T(8,128)(2,1)}, bf16[128,320]{0,1:T(8,128)(2,1)}, u32[]{:S(2)}, u32[]{:S(2)}) collective-permute-start(bf16[128,320]{0,1:T(8,128)(2,1)} %fusion.161), channel_id=1, source_target_pairs={{4,0},{8,4},{12,8},{16,12},{20,16},{24,20},{28,24},{5,1},{9,5},{13... | collective-permute-start | bytes 245768 | tf_op jit(solution)/shard_map/while/body/eval_jaxpr/ppermute | solution.py:12
  380.5 10.2 %collective-permute-start.3 = (bf16[4,128,320]{1,2,0:T(8,128)(2,1)}, bf16[4,128,320]{1,2,0:T(8,128)(2,1)}, u32[]{:S(2)}, u32[]{:S(2)}) collective-permute-start(bf16[4,128,320]{1,2,0:T(8,128)(2,1)} %fusion.162), channel_id=1, source_target_pairs={{4,0},{8,4},{12,8},{16,12},{20,16},{24,20},{28,24},{5,1},{9,5},{13... | collective-permute-start | bytes 983048 | tf_op jit(solution)/shard_map/while/body/eval_jaxpr/ppermute | solution.py:12
  397.7 17.1 %collective-permute-start.2 = (bf16[128,320]{0,1:T(8,128)(2,1)}, bf16[128,320]{0,1:T(8,128)(2,1)}, u32[]{:S(2)}, u32[]{:S(2)}) collective-permute-start(bf16[128,320]{0,1:T(8,128)(2,1)} %fusion.161), channel_id=1, source_target_pairs={{4,0},{8,4},{12,8},{16,12},{20,16},{24,20},{28,24},{5,1},{9,5},{13... | collective-permute-start | bytes 245768 | tf_op jit(solution)/shard_map/while/body/eval_jaxpr/ppermute | solution.py:12
  402.9 10.2 %collective-permute-start.3 = (bf16[4,128,320]{1,2,0:T(8,128)(2,1)}, bf16[4,128,320]{1,2,0:T(8,128)(2,1)}, u32[]{:S(2)}, u32[]{:S(2)}) collective-permute-start(bf16[4,128,320]{1,2,0:T(8,128)(2,1)} %fusion.162), channel_id=1, source_target_pairs={{4,0},{8,4},{12,8},{16,12},{20,16},{24,20},{28,24},{5,1},{9,5},{13... | collective-permute-start | bytes 983048 | tf_op jit(solution)/shard_map/while/body/eval_jaxpr/ppermute | solution.py:12
  420.1 17.1 %collective-permute-start.2 = (bf16[128,320]{0,1:T(8,128)(2,1)}, bf16[128,320]{0,1:T(8,128)(2,1)}, u32[]{:S(2)}, u32[]{:S(2)}) collective-permute-start(bf16[128,320]{0,1:T(8,128)(2,1)} %fusion.161), channel_id=1, source_target_pairs={{4,0},{8,4},{12,8},{16,12},{20,16},{24,20},{28,24},{5,1},{9,5},{13... | collective-permute-start | bytes 245768 | tf_op jit(solution)/shard_map/while/body/eval_jaxpr/ppermute | solution.py:12
  425.3 10.2 %collective-permute-start.3 = (bf16[4,128,320]{1,2,0:T(8,128)(2,1)}, bf16[4,128,320]{1,2,0:T(8,128)(2,1)}, u32[]{:S(2)}, u32[]{:S(2)}) collective-permute-start(bf16[4,128,320]{1,2,0:T(8,128)(2,1)} %fusion.162), channel_id=1, source_target_pairs={{4,0},{8,4},{12,8},{16,12},{20,16},{24,20},{28,24},{5,1},{9,5},{13... | collective-permute-start | bytes 983048 | tf_op jit(solution)/shard_map/while/body/eval_jaxpr/ppermute | solution.py:12
  442.6 17.1 %collective-permute-start.2 = (bf16[128,320]{0,1:T(8,128)(2,1)}, bf16[128,320]{0,1:T(8,128)(2,1)}, u32[]{:S(2)}, u32[]{:S(2)}) collective-permute-start(bf16[128,320]{0,1:T(8,128)(2,1)} %fusion.161), channel_id=1, source_target_pairs={{4,0},{8,4},{12,8},{16,12},{20,16},{24,20},{28,24},{5,1},{9,5},{13... | collective-permute-start | bytes 245768 | tf_op jit(solution)/shard_map/while/body/eval_jaxpr/ppermute | solution.py:12
  447.8 10.2 %collective-permute-start.3 = (bf16[4,128,320]{1,2,0:T(8,128)(2,1)}, bf16[4,128,320]{1,2,0:T(8,128)(2,1)}, u32[]{:S(2)}, u32[]{:S(2)}) collective-permute-start(bf16[4,128,320]{1,2,0:T(8,128)(2,1)} %fusion.162), channel_id=1, source_target_pairs={{4,0},{8,4},{12,8},{16,12},{20,16},{24,20},{28,24},{5,1},{9,5},{13... | collective-permute-start | bytes 983048 | tf_op jit(solution)/shard_map/while/body/eval_jaxpr/ppermute | solution.py:12
  465.0 17.1 %collective-permute-start.2 = (bf16[128,320]{0,1:T(8,128)(2,1)}, bf16[128,320]{0,1:T(8,128)(2,1)}, u32[]{:S(2)}, u32[]{:S(2)}) collective-permute-start(bf16[128,320]{0,1:T(8,128)(2,1)} %fusion.161), channel_id=1, source_target_pairs={{4,0},{8,4},{12,8},{16,12},{20,16},{24,20},{28,24},{5,1},{9,5},{13... | collective-permute-start | bytes 245768 | tf_op jit(solution)/shard_map/while/body/eval_jaxpr/ppermute | solution.py:12
  470.2 10.2 %collective-permute-start.3 = (bf16[4,128,320]{1,2,0:T(8,128)(2,1)}, bf16[4,128,320]{1,2,0:T(8,128)(2,1)}, u32[]{:S(2)}, u32[]{:S(2)}) collective-permute-start(bf16[4,128,320]{1,2,0:T(8,128)(2,1)} %fusion.162), channel_id=1, source_target_pairs={{4,0},{8,4},{12,8},{16,12},{20,16},{24,20},{28,24},{5,1},{9,5},{13... | collective-permute-start | bytes 983048 | tf_op jit(solution)/shard_map/while/body/eval_jaxpr/ppermute | solution.py:12
  487.4 17.1 %collective-permute-start.2 = (bf16[128,320]{0,1:T(8,128)(2,1)}, bf16[128,320]{0,1:T(8,128)(2,1)}, u32[]{:S(2)}, u32[]{:S(2)}) collective-permute-start(bf16[128,320]{0,1:T(8,128)(2,1)} %fusion.161), channel_id=1, source_target_pairs={{4,0},{8,4},{12,8},{16,12},{20,16},{24,20},{28,24},{5,1},{9,5},{13... | collective-permute-start | bytes 245768 | tf_op jit(solution)/shard_map/while/body/eval_jaxpr/ppermute | solution.py:12
  (95 other events, 318.6 us)
Sparse Core Ops, SparseCore 0:
  510.8 110.8 all-reduce.2
where the time goes:
time: 644 us; the launch traced here: 635 us
  matrix products  203 us (32%)
  waiting for transfers between devices  166 us (26%)
  local copies, waits for them, and re-layouts  97.3 us (15%)
  starting transfers between devices  86.6 us (13%)
  other arithmetic  64.4 us (10%)
  between operations  16.7 us (3%)
    psum x1, waiting for transfers between devices, local(): lax.psum(totals[0].astype(jnp.bfloat16), 'dp').astype(jnp.float32)  111 us
    ppermute x44, starting transfers between devices, passed_along(): return lax.ppermute(block, axis, route)  86.6 us
    dot_general x33, matrix products, contract_rows(): lax.dot_general(left, right, (((0,), (0,)), ((), ())), preferred_element_...  78.7 us
    ppermute x44, waiting for transfers between devices, passed_along(): return lax.ppermute(block, axis, route)  55.1 us
    while x176, local copies, waits for them, and re-layouts  52.1 us
    dot_general x11, matrix products, inner_block(): jnp.dot(hidden, w_second, preferred_element_type=jnp.float32)  44.1 us
    dot_general x33, matrix products, contract_cols(): lax.dot_general(left, right, (((1,), (1,)), ((), ())), preferred_element_...  35.2 us
    dynamic_slice x22, local copies, waits for them, and re-layouts, keep(): return buffer.at[position].set(jnp.where(flag, value, buffer[position]))  27.2 us
  transfers between devices with their start and end apart: 45, of which 12 were waited for; matrix products, arithmetic and copies ran while one was open for 29% of the time, Pallas kernels for 0%

commit v1 on v0

v1 whole, which is shorter than its diff:
```python
import functools
import math

import jax
import jax.numpy as jnp
from jax import lax
from jax.experimental import pallas as pl
from jax.experimental.pallas import tpu as pltpu
from jax.sharding import PartitionSpec as P

BF16 = jnp.bfloat16
F32 = jnp.float32
GELU_A = math.sqrt(2.0 / math.pi)
GELU_B = 0.044715
PAD = 16
FORWARD_PARTS, BACKWARD_PARTS, WEIGHT_PARTS = 5, 2, 2
IN_HBM = pl.BlockSpec(memory_space=pl.ANY)


def nn(left, right):
    return lax.dot_general(left, right, (((1,), (0,)), ((), ())), preferred_element_type=F32)


def nt(left, right):
    return lax.dot_general(left, right, (((1,), (1,)), ((), ())), preferred_element_type=F32)


def tn(left, right):
    return lax.dot_general(left, right, (((0,), (0,)), ((), ())), preferred_element_type=F32)


def gelu_parts(v):
    square = v * v
    t = jnp.tanh(v * (GELU_A + (GELU_A * GELU_B) * square))
    half = 0.5 + 0.5 * t
    hidden = v * half
    slope = half + hidden * (1.0 - t) * (GELU_A + (3.0 * GELU_A * GELU_B) * square)
    return hidden, slope


def over_columns(total, parts, value, body):
    step = total // parts if total % (parts * 128) == 0 else total
    for start in range(0, total, step):
        value = body(pl.ds(start, step), value)
    return value


def place():
    rank = lax.axis_index("section")
    return lax.div(rank, 2), lax.rem(rank, 2)


def within(stage, stages):
    return (stage >= stages[0]) & (stage <= stages[-1])


def norm_of(merged):
    widened = merged.astype(F32)
    scale = lax.rsqrt(jnp.mean(widened * widened, axis=-1, keepdims=True) + 1e-05)
    return widened, scale


def add_rows(pre, code_rows):
    groups = code_rows.shape[0]
    height = pre.shape[0] // groups
    return jnp.concatenate(
        [pre[i * height : (i + 1) * height] + code_rows[i : i + 1] for i in range(groups)], axis=0
    )


def layer_forward(merged, w_first, w_second, code, slope_out):
    widened, scale = norm_of(merged)
    normed = (widened * scale).astype(BF16)

    def column_part(cols, total):
        pre = add_rows(nn(normed, w_first[:, cols]), code(cols))
        hidden, slope = gelu_parts(pre)
        slope_out[:, cols] = slope.astype(BF16)
        return total + nt(hidden.astype(BF16), w_second[:, cols])

    return over_columns(w_first.shape[1], FORWARD_PARTS, widened, column_part).astype(BF16)


def layer_backward(merged, out_grad, slope, w_first, w_second):
    def column_part(cols, total):
        hidden_grad = nn(out_grad, w_second[:, cols])
        pre_grad = (hidden_grad * slope[:, cols].astype(F32)).astype(BF16)
        return total + nt(pre_grad, w_first[:, cols])

    norm_grad = over_columns(w_first.shape[1], BACKWARD_PARTS, jnp.zeros(out_grad.shape, F32), column_part)
    widened, scale = norm_of(merged[...])
    unit = widened * scale
    inner = jnp.mean(norm_grad * unit, axis=-1, keepdims=True)
    return (out_grad.astype(F32) + scale * (norm_grad - unit * inner)).astype(BF16)


def added(a, b):
    return (a.astype(F32) + b.astype(F32)).astype(BF16)


class Copies:
    def __init__(self, semaphores, core):
        self.semaphores = semaphores
        self.used = 0
        self.core = core

    def start(self, source, target):
        copy = pltpu.make_async_copy(source, target, self.semaphores.at[self.used])
        self.used += 1
        copy.start()
        return copy

    def start_one_of(self, *choices):
        semaphore = self.semaphores.at[self.used]
        self.used += 1
        for flag, source, target in choices:
            pl.when(flag)(pltpu.make_async_copy(source, target, semaphore).start)
        return pltpu.make_async_copy(choices[0][1], choices[0][2], semaphore)

    def start_layer(self, at, own, other, target):
        return self.start_one_of((self.core == at, own, target), (self.core != at, other, target))

    def start_layer_out(self, at, source, own, other):
        return self.start_one_of((self.core == at, source, own), (self.core != at, source, other))


def take_rows(copies, source, target):
    if len(source.shape) == 3:
        groups = target.shape[0]
        return copies.start(source.at[pl.ds(copies.core * groups, groups)], target)
    return copies.start(source, target)


def rows_of(ref):
    if len(ref.shape) == 3:
        return jnp.concatenate([ref[i].astype(F32).T for i in range(ref.shape[0])], axis=0).astype(BF16)
    return ref[...]


def forward_kernel(which, upper, first_stage, n_alias, *refs):
    x, skip_a, skip_b = refs[:3]
    own, other = refs[3:7], refs[7:11]
    refs = refs[11 + n_alias :]
    hop, rows_keep, rows_send, out_a, out_keep, out_send, slopes = refs[:7]
    x_here, rows_here, outs_here, slopes_here, skips_here, first_here, second_here, code_here, merge_here = refs[7:16]
    sized, semaphores = refs[16:]
    groups = sized.shape[0]
    stage, core = place()

    @pl.when(stage == which)
    def _():
        copies = Copies(semaphores, core)
        if upper:
            skip_copies = [copies.start(skip_a, skips_here.at[0])]
        if not (upper and first_stage):
            x_copy = take_rows(copies, x, x_here)
        merge_copies, weight_copies = [], []
        for at in (0, 1):
            if upper:
                merge_copies.append(copies.start_layer(at, own[3], other[3], merge_here.at[at]))
            weight_copies.append(
                [
                    copies.start_layer(at, own[0], other[0], first_here.at[at]),
                    copies.start_layer(at, own[2], other[2], code_here.at[at]),
                    copies.start_layer(at, own[1], other[1], second_here.at[at]),
                ]
            )
            if upper and at == 0:
                skip_copies.append(copies.start(skip_b, skips_here.at[1]))
        finals = []
        for at in (0, 1):
            if at == 0:
                if upper:
                    skip_copies[0].wait()
                if upper and first_stage:
                    arrived = skips_here[0]
                else:
                    x_copy.wait()
                    arrived = rows_of(x_here)
            elif upper:
                skip_copies[1].wait()
            merged = arrived
            if upper:
                merge_copies[at].wait()
                merged = (merged.astype(F32) + nn(skips_here[at], merge_here[at])).astype(BF16)
            rows_here[at] = merged
            finals.append(copies.start_layer_out(at, rows_here.at[at], rows_keep, rows_send))
            for copy in weight_copies[at]:
                copy.wait()

            def code_of(cols):
                both = code_here[at, pl.ds(0, 2 * groups), cols]
                return jnp.where(core == 0, both[:groups], both[groups:])

            result = layer_forward(merged, first_here.at[at], second_here.at[at], code_of, slopes_here.at[at])
            outs_here[at] = result
            finals.append(copies.start(outs_here.at[at], (out_a, hop)[at]))
            finals.append(copies.start_layer_out(at, outs_here.at[at], out_keep, out_send))
            finals.append(copies.start(slopes_here.at[at], slopes.at[at]))
            arrived = result
        for copy in finals:
            copy.wait()


def backward_kernel(which, upper, middle, n_alias, *refs):
    arrived, rows_keep, rows_send, slopes, extra_a, extra_b = refs[:6]
    own, other = refs[6:9], refs[9:12]
    refs = refs[12 + n_alias :]
    hop, kept, sent = refs[:3]
    if upper:
        grads, back_b = refs[3:5]
        refs = refs[5:]
    else:
        refs = refs[3:]
    arrived_here, rows_here, slopes_here, extra_here, grads_here, first_here, second_here, merge_here = refs[:8]
    semaphores = refs[8]
    stage, core = place()

    @pl.when(stage == which)
    def _():
        copies = Copies(semaphores, core)
        arrived_copy = take_rows(copies, arrived, arrived_here)
        layers = (1,) if which == 0 else (1, 0)
        waits = {}
        for at in layers:
            waits[at] = [
                copies.start_layer(at, own[1], other[1], second_here.at[at]),
                copies.start(slopes.at[at], slopes_here.at[at]),
                copies.start_layer(at, own[0], other[0], first_here.at[at]),
                copies.start_layer(at, rows_keep, rows_send, rows_here.at[at]),
            ]
            if middle:
                waits[at].append(copies.start_layer(at, own[2], other[2], merge_here.at[at]))
            elif not upper and at == 1:
                extra_copies = [copies.start(extra_a, extra_here.at[0])]
                if which > 0:
                    extra_copies.append(copies.start(extra_b, extra_here.at[1]))
        arrived_copy.wait()
        out_grad = rows_of(arrived_here)
        grads_here[2] = out_grad
        finals = [copies.start_layer_out(1, grads_here.at[2], kept, sent)]
        for at in (1, 0):
            if at in layers:
                for copy in waits[at]:
                    copy.wait()
                grad = layer_backward(
                    rows_here.at[at], out_grad, slopes_here.at[at], first_here.at[at], second_here.at[at]
                )
            if upper:
                grads_here[at] = grad
                if at == 0 and not middle:
                    finals.append(copies.start(grads_here.at[0], hop))
                if at == 1:
                    finals.append(copies.start_layer_out(0, grads_here.at[1], kept, sent))
                finals.append(copies.start(grads_here.at[at], grads.at[at]))
                if middle:
                    returned = nt(grad, merge_here[at]).astype(BF16)
                    if at == 1:
                        grads_here[3] = returned
                        finals.append(copies.start(grads_here.at[3], back_b))
                    else:
                        grads_here[4] = added(grad, returned)
                        finals.append(copies.start(grads_here.at[4], hop))
                out_grad = grad
            elif at == 1:
                extra_copies[0].wait()
                out_grad = added(grad, extra_here[0])
                grads_here[1] = out_grad
                finals.append(copies.start_layer_out(0, grads_here.at[1], kept, sent))
            elif which > 0:
                extra_copies[1].wait()
                grads_here[0] = added(grad, extra_here[1])
                finals.append(copies.start(grads_here.at[0], hop))
        for copy in finals:
            copy.wait()


def returns_kernel(which, middle, n_alias, *refs):
    grads, skip_a, skip_b, own, other = refs[:5]
    merges, back_a, back_b, grads_here, skips_here, merge_here, merges_here, semaphores = refs[5 + n_alias :]
    stage, core = place()

    @pl.when(stage == which)
    def _():
        copies = Copies(semaphores, core)
        waits = [copies.start(grads, grads_here)]
        for at, skip in ((0, skip_a), (1, skip_b)):
            waits.append(copies.start(skip, skips_here.at[at]))
            waits.append(copies.start_layer(at, own, other, merge_here.at[at]))
        for copy in waits:
            copy.wait()
        finals = []
        for at in (0, 1):
            merges_here[jnp.where(core == at, 1, 0)] = tn(skips_here[at], grads_here[at]).astype(BF16)
        finals.append(copies.start(merges_here, merges))
        if not middle:
            for at, back in ((0, back_a), (1, back_b)):
                skips_here[at] = nt(grads_here[at], merge_here[at]).astype(BF16)
                finals.append(copies.start(skips_here.at[at], back))
        for copy in finals:
            copy.wait()


def weight_kernel(distance, groups, n_before, last, *refs):
    rows, grad, refs = refs[0], refs[1], refs[2:]
    w_first, w_second, w_clock = refs[:3]
    refs = refs[3:]
    before, sums_before = refs[:n_before], refs[n_before : n_before + 2]
    refs = refs[n_before + 2 :]
    if last:
        out_first, out_second, out_clock = refs[:3]
        refs = refs[3:]
    else:
        totals, sums, codes = refs[:3]
        refs = refs[3:]
    rows_here, grads_here, first_here, second_here, clock_here, before_here, results_here = refs[:7]
    sums_here, codes_here, semaphores = refs[7:]
    height = grads_here.shape[0] // 2
    tall = height // groups
    stage, core = place()
    copies = Copies(semaphores, core)
    slot = lax.axis_index("dp") ^ distance
    waits = [
        copies.start(rows.at[slot], rows_here),
        copies.start(w_first, first_here),
        copies.start(w_clock, clock_here),
        copies.start(grad, grads_here),
        copies.start(w_second, second_here),
    ]
    if distance > 0:
        waits.append(copies.start(sums_before[0], sums_here))
        waits.append(copies.start(sums_before[1], codes_here))
    total_copies = [copies.start(ref, before_here.at[i]) for i, ref in enumerate(before)]
    for copy in waits:
        copy.wait()
    table = rows_here[pl.ds(2 * height, PAD), :]
    codes_here[slot] = table
    merged = rows_here[pl.ds(0, 2 * height), :]
    widened, scale = norm_of(merged)
    normed = (widened * scale).astype(BF16)
    out_grad = grads_here[...]
    finals = []

    def column_part(cols, value):
        both = nn(table, clock_here[:, cols])
        own_code = jnp.where(core == 0, both[:groups], both[groups : 2 * groups])
        rest = jnp.where(core == 0, both[groups : 2 * groups], both[:groups])
        pre = add_rows(nn(normed, first_here[:, cols]), jnp.concatenate([own_code, rest], axis=0))
        hidden, slope = gelu_parts(pre)
        pre_grad = (nn(out_grad, second_here[:, cols]) * slope).astype(BF16)
        wide_grad = pre_grad.astype(F32)
        lines = [jnp.sum(wide_grad[i * tall : (i + 1) * tall], axis=0, keepdims=True) for i in range(2 * groups)]
        sums_here[slot, pl.ds(0, 2 * groups), cols] = jnp.concatenate(lines, axis=0)
        for kind, value in ((0, tn(normed, pre_grad)), (1, tn(out_grad, hidden.astype(BF16)))):
            if cols.start == 0 and kind == 0:
                for copy in total_copies:
                    copy.wait()
            for i in range(n_before):
                value = value + before_here[i, kind, :, cols]
            results_here[kind, :, cols] = value

    over_columns(results_here.shape[2], WEIGHT_PARTS, None, column_part)
    if not last:
        finals = [copies.start(results_here, totals), copies.start(sums_here, sums), copies.start(codes_here, codes)]
    else:
        finals = [copies.start(results_here.at[0], out_first), copies.start(results_here.at[1], out_second)]
        total = jnp.zeros(out_clock.shape, F32)
        for replica in range(sums_here.shape[0]):
            table = codes_here[replica]
            mine = jnp.where(core == 0, table[:groups], table[groups : 2 * groups])
            rest = jnp.where(core == 0, table[groups : 2 * groups], table[:groups])
            order = jnp.concatenate([mine, rest], axis=0)
            total = total + tn(order, sums_here[replica, pl.ds(0, 2 * groups), :].astype(BF16))
        before_here[0, 0] = total
        finals.append(copies.start(before_here.at[0, 0], out_clock))
    for copy in finals:
        copy.wait()


def assemble_kernel(turns, n_alias, *refs):
    keep, came = refs[:2]
    result, here, turned, semaphores = refs[2 + n_alias :]
    groups, width, height = turned.shape[1:]
    stage, core = place()
    flags = [within(stage, t) for t in turns]

    @pl.when(functools.reduce(jnp.logical_or, flags))
    def _():
        copies = Copies(semaphores, core)
        waits = [copies.start(keep, here.at[0]), copies.start(came, here.at[1])]
        finals = []
        for i in (0, 1):
            waits[i].wait()
            for g in range(groups):
                turned[i, g] = here[i, pl.ds(g * height, height), :].astype(F32).T.astype(BF16)
            first = core if i == 0 else 1 - core
            finals.append(copies.start(turned.at[i], result.at[pl.ds(first * groups, groups)]))
        for copy in finals:
            copy.wait()


def shape(dims, dtype=BF16):
    return jax.ShapeDtypeStruct(dims, dtype)


def call(kernel, args, outs, scratch, aliases=None, flops=0, name=None):
    return pl.pallas_call(
        kernel,
        out_shape=outs,
        in_specs=[IN_HBM] * len(args),
        out_specs=[IN_HBM] * len(outs),
        scratch_shapes=scratch,
        input_output_aliases=aliases or {},
        compiler_params=pltpu.CompilerParams(vmem_limit_bytes=58 << 20),
        cost_estimate=pl.CostEstimate(flops=flops, bytes_accessed=1, transcendentals=0),
        name=name,
    )(*args)


def embed(step_value, width):
    half_width = width // 2
    position = jnp.arange(half_width).astype(F32)
    frequency = jnp.exp(-math.log(10000.0) * position / half_width)
    angle = step_value.astype(F32)[:, None] * frequency[None, :]
    return jnp.concatenate([jnp.sin(angle), jnp.cos(angle)], axis=1).astype(BF16)


def after(value, *others):
    return lax.optimization_barrier((value,) + others)[0]


def local(latents, steps, cotangent, w_in, w_out, w_time, w_skip):
    sections = lax.axis_size("section")
    replicas = lax.axis_size("dp")
    stages = sections // 2
    half = stages // 2
    rank = lax.axis_index("section")
    core = rank % 2
    micro, height, width = latents.shape
    groups = micro // 2
    rows = groups * height
    hidden = w_in.shape[2]
    w_first = w_in[0]
    w_second = w_out[0].T
    w_clock = w_time[0]
    w_merge = w_skip[0]

    def swap_cores(block):
        return lax.ppermute(block, "section", [(i, i ^ 1) for i in range(sections)])

    def hop_between(block, low):
        pairs = {}
        for first in range(low % 2, stages - 1, 2):
            pairs[first], pairs[first + 1] = first + 1, first
        return lax.ppermute(
            block, "section", [(2 * a + c, 2 * b + c) for a, b in pairs.items() for c in (0, 1)]
        )

    def between(block, a, b):
        pairs = [(a, b), (b, a)]
        return lax.ppermute(block, "section", [(2 * i + c, 2 * j + c) for i, j in pairs for c in (0, 1)])

    def over_replicas(block, distance, which_stages):
        route = []
        for stage in which_stages:
            for c in (0, 1):
                base = (2 * stage + c) * replicas
                route += [(base + z, base + (z ^ distance)) for z in range(replicas)]
        return lax.ppermute(block, ("section", "dp"), route)

    distances = sorted(range(1, replicas), key=lambda d: (d != 1, -d))
    low_stages, high_stages = range(half), range(half, stages)

    other_first = swap_cores(w_first)
    table = embed(steps[0], width)
    table = jnp.concatenate([table, jnp.zeros((PAD - micro, width), BF16)], axis=0)
    code = nn(table, w_clock)
    other_code = swap_cores(code)
    other_second = swap_cores(w_second)
    other_merge = swap_cores(w_merge)

    flops = 0
    weight_flops = 4 * rows * width * hidden
    block, two_blocks = (rows, width), (2, rows, width)
    slopes = (2, rows, hidden)
    native = (groups, width, height)
    group_marker = pltpu.VMEM((groups, 128), F32)
    two_weights = [pltpu.VMEM((2, width, hidden), BF16)] * 2
    merge_pair = (2, width, width)

    saved = {}

    def forward(stage, x, skips):
        upper, first_stage = stage >= half, stage in (0, half)
        args = [x, *(skips or (table, table))]
        args += [w_first, w_second, code, w_merge, other_first, other_second, other_code, other_merge]
        keys = ("keep", "send", ("a", stage), "out_keep", "out_send", "slopes")
        aliases = {}
        for output, key in enumerate(keys):
            if key in saved:
                aliases[len(args)] = 1 + output
                args.append(saved[key])
        scratch = [pltpu.VMEM(native if x.ndim == 3 else block, BF16), pltpu.VMEM(two_blocks, BF16)]
        scratch += [pltpu.VMEM(two_blocks, BF16), pltpu.VMEM(slopes, BF16), pltpu.VMEM(two_blocks, BF16)]
        scratch += two_weights + [pltpu.VMEM((2, PAD, hidden), F32), pltpu.VMEM(merge_pair, BF16)]
        scratch += [group_marker, pltpu.SemaphoreType.DMA((24,))]
        result = call(
            functools.partial(forward_kernel, stage, upper, first_stage, len(aliases)),
            args, [shape(block)] * 6 + [shape(slopes)], scratch, aliases, flops, f"forward_stage_{stage}",
        )
        saved.update(zip(keys, result[1:]))
        return result[0]

    x = latents.transpose(0, 2, 1)
    skips = {}
    for stage in range(stages):
        sent = forward(stage, x, skips.get(stage))
        if stage < stages - 1 and stage != half - 1:
            x = hop_between(sent, stage)
        if stage < half:
            up = stages - 1 - stage
            skips[up] = (between(sent, stage, up), between(saved["a", stage], stage, up))
            if stage == half - 1:
                x = skips[up][0]

    weights_of = [w_first, w_second, w_merge, other_first, other_second, other_merge]
    back_pairs = {}
    arrived = cotangent.transpose(0, 2, 1)
    kept = []
    merges = None

    def backward_scratch():
        scratch = [pltpu.VMEM(native if arrived.ndim == 3 else block, BF16), pltpu.VMEM(two_blocks, BF16)]
        scratch += [pltpu.VMEM(slopes, BF16), pltpu.VMEM(two_blocks, BF16)]
        scratch += [pltpu.VMEM((5,) + block, BF16)] + two_weights
        scratch += [pltpu.VMEM(merge_pair, BF16), pltpu.SemaphoreType.DMA((24,))]
        return scratch

    def returns(stage, grads, waited):
        args = [after(grads, waited), *skips[stage], w_merge, other_merge]
        aliases = {}
        if merges is not None:
            aliases = {len(args): 0}
            args.append(merges)
        scratch = [pltpu.VMEM(two_blocks, BF16)] * 2 + [pltpu.VMEM(merge_pair, BF16)] * 2
        return call(
            functools.partial(returns_kernel, stage, stage == half, len(aliases)),
            args, [shape(merge_pair), shape(block), shape(block)], scratch + [pltpu.SemaphoreType.DMA((12,))],
            aliases, flops // 4, f"returns_stage_{stage}",
        )

    for stage in range(stages - 1, half - 1, -1):
        middle = stage == half
        args = [arrived, saved["keep"], saved["send"], saved["slopes"], arrived, arrived] + weights_of
        aliases = {len(args) + i: 1 + i for i in range(len(kept))}
        args += kept
        sent, *kept, grads, back_b = call(
            functools.partial(backward_kernel, stage, True, middle, len(aliases)),
            args, [shape(block)] * 3 + [shape(two_blocks), shape(block)], backward_scratch(),
            aliases, flops, f"backward_stage_{stage}",
        )
        low = stages - 1 - stage
        if middle:
            sent = after(sent, *[value for pair in back_pairs.values() for value in pair])
            arrived = between(sent, half, half - 1)
            back_pairs[low] = (None, between(after(back_b, sent), half, half - 1))
            middle_grads = grads
        else:
            arrived = hop_between(sent, stage - 1)
            merges, back_a, back_b = returns(stage, grads, sent)
            back_pairs[low] = (between(back_a, stage, low + 1), between(back_b, stage, low))
            if stage == stages - 1:
                came = swap_cores(after(saved["send"], back_b))
                packed = jnp.concatenate([saved["keep"], came, table], axis=0)
                gathered = lax.all_gather(packed, "dp")
                came = swap_cores(after(saved["out_send"], packed))
                arrived = after(arrived, came)

    def assemble(turns, before, waited):
        args = [after(saved["out_keep"], waited), came] + ([] if before is None else [before])
        return call(
            functools.partial(assemble_kernel, turns, len(args) - 2),
            args, [shape((micro, width, height))],
            [pltpu.VMEM(two_blocks, BF16), pltpu.VMEM((2,) + native, BF16), pltpu.SemaphoreType.DMA((8,))],
            {} if before is None else {2: 0}, flops // 8, "outputs_" + "_".join(str(t[0]) for t in turns),
        )[0]

    outputs = assemble([(0, 0), (half, stages - 1)], None, sent)

    def merge_gradients():
        total = (merges[1].astype(F32) + swap_cores(merges[0]).astype(F32)).astype(BF16)
        distance = 1
        while distance < replicas:
            came = over_replicas(total, distance, high_stages)
            total = (total.astype(F32) + came.astype(F32)).astype(BF16)
            distance *= 2
        return jnp.where(rank // 2 < half, 0.0, total.astype(F32))

    for stage in range(half - 1, -1, -1):
        extra_b = back_pairs[stage - 1][0] if stage > 0 else arrived
        args = [after(arrived, outputs), saved["keep"], saved["send"], saved["slopes"]]
        args += [back_pairs[stage][1], extra_b] + weights_of
        aliases = {len(args) + i: 1 + i for i in range(2)}
        sent, *kept = call(
            functools.partial(backward_kernel, stage, False, False, 2),
            args + kept, [shape(block)] * 3, backward_scratch(), aliases, flops, f"backward_stage_{stage}",
        )
        if stage > 0:
            arrived = hop_between(sent, stage - 1)
        if stage == 1:
            merges = returns(half, middle_grads, sent)[0]
            grad_merge = merge_gradients()
            arrived = after(arrived, grad_merge, gathered)

    kept_grad, sent_grad = kept
    came_grad = swap_cores(sent_grad)
    grad = jnp.concatenate([kept_grad, came_grad], axis=0)
    grads = {d: over_replicas(grad, d, range(stages)) for d in distances}
    grads[0] = grad
    outputs = assemble([(1, half - 1)], outputs, grads[1])
    matrices, lines, codes = (2, width, hidden), (replicas, PAD, hidden), (replicas, PAD, width)

    def weights(d, before, sums, last):
        args = [gathered, grads[d], w_first, w_second, w_clock, *before, *sums]
        outs = [shape(matrices, F32), shape(lines, F32), shape(codes)]
        if last:
            outs = [shape((width, hidden), F32)] * 3
        scratch = [pltpu.VMEM((2 * rows + PAD, width), BF16), pltpu.VMEM((2 * rows, width), BF16)]
        scratch += [pltpu.VMEM((width, hidden), BF16)] * 3
        scratch += [pltpu.VMEM((max(1, len(before)),) + matrices, F32), pltpu.VMEM(matrices, F32)]
        scratch += [pltpu.VMEM(lines, F32), pltpu.VMEM(codes, BF16), pltpu.SemaphoreType.DMA((16,))]
        return call(
            functools.partial(weight_kernel, d, groups, len(before), last),
            args, outs, scratch, None, weight_flops, f"weights_{d}",
        )

    stack = []
    sums = (table, table)
    order = [0] + distances if replicas == 4 else list(range(replicas))
    for count, d in enumerate(order):
        before = []
        number = count + 1
        while number % 2 == 0:
            before.append(stack.pop())
            number //= 2
        last = count == replicas - 1
        result = weights(d, before, sums, last)
        if not last:
            stack.append(result[0])
            sums = tuple(result[1:])
    grad_first, grad_second, grad_clock = result

    return (
        outputs.transpose(0, 2, 1)[None],
        grad_first[None],
        grad_second.T[None],
        grad_clock[None],
        grad_merge[None],
    )


def solution(mesh):
    placed = (
        P(None, "dp", None),
        P("dp", None),
        P(None, "dp", None),
        P("section", None, None),
        P("section", None, None),
        P("section", None, None),
        P("section", None, None),
    )
    return jax.shard_map(
        local,
        mesh=mesh,
        in_specs=placed,
        out_specs=(
            P("section", None, "dp", None),
            P("section", None, None),
            P("section", None, None),
            P("section", None, None),
            P("section", None, None),
        ),
        check_vma=False,
    )
```

time: 644 us -> 189 us (0.29); the launches traced: 635 us -> 188 us
  matrix products: 203 us -> 1.41 us
  waiting for transfers between devices: 166 us -> 58.8 us
  local copies, waits for them, and re-layouts: 97.3 us -> 9.86 us
  other arithmetic: 64.4 us -> 4.31 us
  Pallas kernels: 0 us -> 48.4 us
  starting transfers between devices: 86.6 us -> 51 us
    dot_general x121 -> x1, matrix products: 203 us -> 1.41 us  [nn(): lax.dot_general(left, right, (((1,), (0,)), ((), ())), preferred_element_...]
    psum x1 -> x0, waiting for transfers between devices: 111 us -> none  [local(): lax.psum(totals[0].astype(jnp.bfloat16), 'dp').astype(jnp.float32)]
    while x176 -> x0, local copies, waits for them, and re-layouts: 52.1 us -> none
    pallas_call x0 -> x16, Pallas kernels: none -> 48.4 us  [call(): pl.pallas_call(kernel, out_shape=outs, in_specs=[IN_HBM] * len(args), out...]
    dynamic_slice x44 -> x0, local copies, waits for them, and re-layouts: 37.4 us -> none  [the longest x22 27.2 us: keep(): return buffer.at[position].set(jnp.where(flag, value, buffer[position]))]
    ppermute x44 -> x25, starting transfers between devices: 86.6 us -> 50.9 us  [the longest x8 21.8 us: between(): lax.ppermute(block, 'section', [(2 * i + c, 2 * j + c) for i, j in pairs...]
    scatter x11 -> x0, other arithmetic: 17.3 us -> none  [keep(): return buffer.at[position].set(jnp.where(flag, value, buffer[position]))]
    broadcast_in_dim x8 -> x0, other arithmetic: 12.9 us -> none  [the longest x2 4.82 us: local(): summed[0][None]]
  transfers between devices with their start and end apart: 45 -> 26, of which waited for: 12 -> 16; matrix products, arithmetic and copies ran while one was open for 29% -> 4% of each run, Pallas kernels for 0% -> 20%
where the time goes in v1:
time: 189 us; the launch traced here: 188 us
  waiting for transfers between devices  58.8 us (31%)
  starting transfers between devices  51 us (27%)
  Pallas kernels  48.4 us (26%)
  between operations  14.5 us (8%)
  local copies, waits for them, and re-layouts  9.86 us (5%)
  other arithmetic  4.31 us (2%)
    pallas_call x16, Pallas kernels, call(): pl.pallas_call(kernel, out_shape=outs, in_specs=[IN_HBM] * len(args), out...  48.4 us
    ppermute x5, waiting for transfers between devices, over_replicas(): return lax.ppermute(block, ('section', 'dp'), route)  28.6 us
    ppermute x8, starting transfers between devices, between(): lax.ppermute(block, 'section', [(2 * i + c, 2 * j + c) for i, j in pairs...  21.8 us
    ppermute x4, waiting for transfers between devices, hop_between(): lax.ppermute(block, 'section', [(2 * a + c, 2 * b + c) for a, b in pairs....  15.6 us
    ppermute x4, starting transfers between devices, hop_between(): lax.ppermute(block, 'section', [(2 * a + c, 2 * b + c) for a, b in pairs....  14.7 us
    ppermute x5, starting transfers between devices, over_replicas(): return lax.ppermute(block, ('section', 'dp'), route)  13.2 us
    ppermute x8, waiting for transfers between devices, between(): lax.ppermute(block, 'section', [(2 * i + c, 2 * j + c) for i, j in pairs...  10.8 us
    unnamed x59, local copies, waits for them, and re-layouts  8.77 us
  transfers between devices with their start and end apart: 26, of which 16 were waited for; matrix products, arithmetic and copies ran while one was open for 4% of the time, Pallas kernels for 20%

profile of v1, /device:TPU:4, one launch (start us, length us, event | category | flops | bytes accessed | tf_op | source)
XLA Modules:
  0.0 188.4 jit_solution(13017223885868387898)
XLA Ops:
  8.7 1.4 fusion.6.refs_5_
  13.0 1.6 collective-permute-start.4
  14.5 5.9 %collective-permute-done.4.refs_0_ = bf16[256,320]{1,0:T(8,128)(2,1)S(1)} collective-permute-done((bf16[256,320]{1,0:T(8,128)(2,1)}, bf16[256,320]{1,0:T(8,128)(2,1)S(1)}, u32[]{:S(2)}, u32[]{:S(2)}) %collective-permute-start.4) | collective-permute-done | bytes 163872 | tf_op jit(solution)/shard_map/ppermute | solution.py:455
  21.3 10.4 %collective-permute-start.5 = (bf16[256,320]{1,0:T(8,128)(2,1)}, bf16[256,320]{1,0:T(8,128)(2,1)S(1)}, u32[]{:S(2)}, u32[]{:S(2)}) collective-permute-start(bf16[256,320]{1,0:T(8,128)(2,1)} %get-tuple-element.78), channel_id=1, source_target_pairs={{8,16},{12,20},{16,8},{20,12},{9,17},{13,21},{17,9},{21,13},{10,18... | collective-permute-start | bytes 491528 | tf_op jit(solution)/shard_map/ppermute | solution.py:461
  31.8 1.9 %collective-permute-start.6 = (bf16[256,320]{1,0:T(8,128)(2,1)}, bf16[256,320]{1,0:T(8,128)(2,1)S(1)}, u32[]{:S(2)}, u32[]{:S(2)}) collective-permute-start(bf16[256,320]{1,0:T(8,128)(2,1)} %get-tuple-element.79), channel_id=1, source_target_pairs={{8,16},{12,20},{16,8},{20,12},{9,17},{13,21},{17,9},{21,13},{10,18... | collective-permute-start | bytes 491528 | tf_op jit(solution)/shard_map/ppermute | solution.py:461
  35.1 2.3 %collective-permute-done.5.refs_0_.refs_1_ = bf16[256,320]{1,0:T(8,128)(2,1)S(1)} collective-permute-done((bf16[256,320]{1,0:T(8,128)(2,1)}, bf16[256,320]{1,0:T(8,128)(2,1)S(1)}, u32[]{:S(2)}, u32[]{:S(2)}) %collective-permute-start.5) | collective-permute-done | bytes 163872 | tf_op jit(solution)/shard_map/ppermute | solution.py:461
  37.4 3.5 %collective-permute-done.6.refs_2_ = bf16[256,320]{1,0:T(8,128)(2,1)S(1)} collective-permute-done((bf16[256,320]{1,0:T(8,128)(2,1)}, bf16[256,320]{1,0:T(8,128)(2,1)S(1)}, u32[]{:S(2)}, u32[]{:S(2)}) %collective-permute-start.6) | collective-permute-done | bytes 163872 | tf_op jit(solution)/shard_map/ppermute | solution.py:461
  41.6 5.4 %forward_stage_2.1 = (bf16[256,320]{1,0:T(8,128)(2,1)}, bf16[256,320]{1,0:T(8,128)(2,1)}, bf16[256,320]{1,0:T(8,128)(2,1)}, bf16[256,320]{1,0:T(8,128)(2,1)}, bf...) custom-call(bf16[256,320]{1,0:T(8,128)(2,1)} %copy-done.8, ...), custom_call_target="tpu_custom_call", output_to_operand_aliasing={{1}: (11, {}), {2}: (12, {}), {4}: (13, {}), {5}: (14, {}),... | custom-call | bytes 1 | tf_op jit(solution)/shard_map/forward_stage_2/pallas_call | solution.py:407
  47.2 5.8 %collective-permute-done.7.refs_0_ = bf16[256,320]{1,0:T(8,128)(2,1)S(1)} collective-permute-done((bf16[256,320]{1,0:T(8,128)(2,1)}, bf16[256,320]{1,0:T(8,128)(2,1)S(1)}, u32[]{:S(2)}, u32[]{:S(2)}) %collective-permute-start.7) | collective-permute-done | bytes 163872 | tf_op jit(solution)/shard_map/ppermute | solution.py:455
  54.9 1.4 collective-permute-done.11
  57.2 13.0 %collective-permute-start.10 = (bf16[256,320]{1,0:T(8,128)(2,1)S(1)}, bf16[256,320]{1,0:T(8,128)(2,1)S(1)}, u32[]{:S(2)}, u32[]{:S(2)}) collective-permute-start(bf16[256,320]{1,0:T(8,128)(2,1)S(1)} %copy-done.28), channel_id=1, source_target_pairs={{0,8},{4,12},{8,0},{12,4},{16,24},{20,28},{24,16},{28,20},{1,9},{5... | collective-permute-start | bytes 491528 | tf_op jit(solution)/shard_map/ppermute | solution.py:455
  71.6 3.8 %collective-permute-done.10.refs_0_.refs_4_.refs_5_ = bf16[256,320]{1,0:T(8,128)(2,1)S(1)} collective-permute-done((bf16[256,320]{1,0:T(8,128)(2,1)S(1)}, bf16[256,320]{1,0:T(8,128)(2,1)S(1)}, u32[]{:S(2)}, u32[]{:S(2)}) %collective-permute-start.10) | collective-permute-done | bytes 163872 | tf_op jit(solution)/shard_map/ppermute | solution.py:455
  76.1 5.3 %backward_stage_2.1 = (bf16[256,320]{1,0:T(8,128)(2,1)}, bf16[256,320]{1,0:T(8,128)(2,1)}, bf16[256,320]{1,0:T(8,128)(2,1)}, bf16[2,256,320]{2,1,0:T(8,128)(2,1)}, bf16[256,320]{1,0:T(8,128)(2,1)}) custom-call(bf16[256,320]{1,0:T(8,128)(2,1)} %copy-done.6, ...), custom_call_target="tpu_custom_call", output_to_operand_aliasing={{1}: (12, {}), {2}: (13, {})} | custom-call | bytes 1 | tf_op jit(solution)/shard_map/backward_stage_2/pallas_call | solution.py:407
  81.5 3.5 %collective-permute-start.15 = (bf16[256,320]{1,0:T(8,128)(2,1)}, bf16[256,320]{1,0:T(8,128)(2,1)S(1)}, u32[]{:S(2)}, u32[]{:S(2)}) collective-permute-start(bf16[256,320]{1,0:T(8,128)(2,1)} %get-tuple-element.108), channel_id=1, source_target_pairs={{16,8},{20,12},{8,16},{12,20},{17,9},{21,13},{9,17},{13,21},{18,10... | collective-permute-start | bytes 491528 | tf_op jit(solution)/shard_map/ppermute | solution.py:461
  85.0 3.3 %collective-permute-start.16 = (bf16[256,320]{1,0:T(8,128)(2,1)}, bf16[256,320]{1,0:T(8,128)(2,1)S(1)}, u32[]{:S(2)}, u32[]{:S(2)}) collective-permute-start(bf16[256,320]{1,0:T(8,128)(2,1)} %get-tuple-element.112), channel_id=1, source_target_pairs={{16,8},{20,12},{8,16},{12,20},{17,9},{21,13},{9,17},{13,21},{18,10... | collective-permute-start | bytes 491528 | tf_op jit(solution)/shard_map/ppermute | solution.py:461
  88.3 2.0 %outputs_0_2.1.refs_2_ = bf16[4,320,128]{2,1,0:T(8,128)(2,1)} custom-call(bf16[256,320]{1,0:T(8,128)(2,1)} %get-tuple-element.126.refs_0_, bf16[256,320]{1,0:T(8,128)(2,1)} %copy-done.15), custom_call_target="tpu_custom_call" | custom-call | bytes 1 | tf_op jit(solution)/shard_map/outputs_0_2/pallas_call | solution.py:407
  90.2 1.9 collective-permute-done.15.refs_0_
  92.1 3.0 %collective-permute-done.16.refs_4_ = bf16[256,320]{1,0:T(8,128)(2,1)S(1)} collective-permute-done((bf16[256,320]{1,0:T(8,128)(2,1)}, bf16[256,320]{1,0:T(8,128)(2,1)S(1)}, u32[]{:S(2)}, u32[]{:S(2)}) %collective-permute-start.16) | collective-permute-done | bytes 163872 | tf_op jit(solution)/shard_map/ppermute | solution.py:461
  96.1 2.6 %returns_stage_2.1 = (bf16[2,320,320]{2,1,0:T(8,128)(2,1)}, bf16[256,320]{1,0:T(8,128)(2,1)}, bf16[256,320]{1,0:T(8,128)(2,1)}) custom-call(bf16[2,256,320]{2,1,0:T(8,128)(2,1)} %get-tuple-element.117.refs_0_, bf16[256,320]{1,0:T(8,128)(2,1)} %copy-done.8, bf16[256,320]{1,0:T(8,128)(2,1)} %copy-done.12, ...), custom_call_target="tpu_custom_call", output_to_operand_aliasing={{0}: (5, {})} | custom-call | bytes 1 | tf_op jit(solution)/shard_map/returns_stage_2/pallas_call | solution.py:407
  99.7 1.5 collective-permute-done.18
  101.2 1.0 fusion
  102.2 5.2 %collective-permute-start.19 = (bf16[320,320]{1,0:T(8,128)(2,1)S(1)}, bf16[320,320]{1,0:T(8,128)(2,1)S(1)}, u32[]{:S(2)}, u32[]{:S(2)}) collective-permute-start(bf16[320,320]{1,0:T(8,128)(2,1)S(1)} %fusion), channel_id=1, source_target_pairs={{16,17},{17,16},{18,19},{19,18},{20,21},{21,20},{22,23},{23,22},{2... | collective-permute-start | bytes 614408 | tf_op jit(solution)/shard_map/ppermute | solution.py:469
  107.4 6.5 %collective-permute-done.19 = bf16[320,320]{1,0:T(8,128)(2,1)S(1)} collective-permute-done((bf16[320,320]{1,0:T(8,128)(2,1)S(1)}, bf16[320,320]{1,0:T(8,128)(2,1)S(1)}, u32[]{:S(2)}, u32[]{:S(2)}) %collective-permute-start.19) | collective-permute-done | bytes 204832 | tf_op jit(solution)/shard_map/ppermute | solution.py:469
  114.0 4.4 %collective-permute-start.20 = (bf16[320,320]{1,0:T(8,128)(2,1)S(1)}, bf16[320,320]{1,0:T(8,128)(2,1)S(1)}, u32[]{:S(2)}, u32[]{:S(2)}) collective-permute-start(bf16[320,320]{1,0:T(8,128)(2,1)S(1)} %add_convert_fusion.1), channel_id=1, source_target_pairs={{16,18},{17,19},{18,16},{19,17},{20,22},{21,23},{22,20},{23,21},{2... | collective-permute-start | bytes 614408 | tf_op jit(solution)/shard_map/ppermute | solution.py:469
  118.5 11.2 %collective-permute-done.20 = bf16[320,320]{1,0:T(8,128)(2,1)S(1)} collective-permute-done((bf16[320,320]{1,0:T(8,128)(2,1)S(1)}, bf16[320,320]{1,0:T(8,128)(2,1)S(1)}, u32[]{:S(2)}, u32[]{:S(2)}) %collective-permute-start.20) | collective-permute-done | bytes 204832 | tf_op jit(solution)/shard_map/ppermute | solution.py:469
  133.4 2.9 %collective-permute-start.24 = (bf16[512,320]{1,0:T(8,128)(2,1)S(1)}, bf16[512,320]{1,0:T(8,128)(2,1)S(1)}, u32[]{:S(2)}, u32[]{:S(2)}) collective-permute-start(bf16[512,320]{1,0:T(8,128)(2,1)S(1)} %constant_dynamic-update-slice_fusion.refs_1_), channel_id=1, source_target_pairs={{0,3},{1,2},{2,1},{3,0},{4,7},{5,6},{6,5},{7,4},{8,11},{9,10},{10,... | collective-permute-start | bytes 983048 | tf_op jit(solution)/shard_map/ppermute | solution.py:469
  136.8 7.2 %weights_0.1 = (f32[2,320,1280]{2,1,0:T(8,128)}, f32[4,16,1280]{2,1,0:T(8,128)}, bf16[4,16,320]{2,1,0:T(8,128)(2,1)}) custom-call(bf16[4,528,320]{2,1,0:T(8,128)(2,1)} %bitcast.53, bf16[512,320]{1,0:T(8,128)(2,1)} %copy-done.10, bf16[320,1280]{1,0:T(8,128)(2,1)} %bitcast.36, bf16[320,1280]{1,0:T(8,128)(2,1)} %bitcast.49, bf16[320,1280]{1,0:T(8,128)(2,1)} %bitcast.68, ...), custom_call_target="tpu_custom_call" | custom-call | flops 419430400 | bytes 1 | tf_op jit(solution)/shard_map/weights_0/pallas_call | solution.py:407
  145.2 7.5 %weights_1.1 = (f32[2,320,1280]{2,1,0:T(8,128)}, f32[4,16,1280]{2,1,0:T(8,128)}, bf16[4,16,320]{2,1,0:T(8,128)(2,1)}) custom-call(bf16[4,528,320]{2,1,0:T(8,128)(2,1)} %bitcast.54, bf16[512,320]{1,0:T(8,128)(2,1)} %copy-done.17, bf16[320,1280]{1,0:T(8,128)(2,1)} %bitcast.37, bf16[320,1280]{1,0:T(8,128)(2,1)} %bitcast.50, bf16[320,1280]{1,0:T(8,128)(2,1)} %bitcast.69, ...), custom_call_target="tpu_custom_call" | custom-call | flops 419430400 | bytes 1 | tf_op jit(solution)/shard_map/weights_1/pallas_call | solution.py:407
  152.7 2.0 %collective-permute-done.24.refs_1_ = bf16[512,320]{1,0:T(8,128)(2,1)S(1)} collective-permute-done((bf16[512,320]{1,0:T(8,128)(2,1)S(1)}, bf16[512,320]{1,0:T(8,128)(2,1)S(1)}, u32[]{:S(2)}, u32[]{:S(2)}) %collective-permute-start.24) | collective-permute-done | bytes 327712 | tf_op jit(solution)/shard_map/ppermute | solution.py:469
  155.4 7.3 %weights_3.1 = (f32[2,320,1280]{2,1,0:T(8,128)}, f32[4,16,1280]{2,1,0:T(8,128)}, bf16[4,16,320]{2,1,0:T(8,128)(2,1)}) custom-call(bf16[4,528,320]{2,1,0:T(8,128)(2,1)} %bitcast.55, bf16[512,320]{1,0:T(8,128)(2,1)} %copy-done.18, bf16[320,1280]{1,0:T(8,128)(2,1)} %bitcast.38, bf16[320,1280]{1,0:T(8,128)(2,1)} %bitcast.51, bf16[320,1280]{1,0:T(8,128)(2,1)} %bitcast.70, ...), custom_call_target="tpu_custom_call" | custom-call | flops 419430400 | bytes 1 | tf_op jit(solution)/shard_map/weights_3/pallas_call | solution.py:407
  162.7 8.5 %collective-permute-done.23.refs_1_ = bf16[512,320]{1,0:T(8,128)(2,1)S(1)} collective-permute-done((bf16[512,320]{1,0:T(8,128)(2,1)S(1)}, bf16[512,320]{1,0:T(8,128)(2,1)S(1)}, u32[]{:S(2)}, u32[]{:S(2)}) %collective-permute-start.23) | collective-permute-done | bytes 327712 | tf_op jit(solution)/shard_map/ppermute | solution.py:469
  172.0 9.5 %weights_2.1 = (f32[320,1280]{1,0:T(8,128)}, f32[320,1280]{1,0:T(8,128)}, f32[320,1280]{1,0:T(8,128)}) custom-call(bf16[4,528,320]{2,1,0:T(8,128)(2,1)} %bitcast.56, bf16[512,320]{1,0:T(8,128)(2,1)} %copy-done.16, bf16[320,1280]{1,0:T(8,128)(2,1)} %bitcast.39, bf16[320,1280]{1,0:T(8,128)(2,1)} %bitcast.52, bf16[320,1280]{1,0:T(8,128)(2,1)} %bitcast.71, ...), custom_call_target="tpu_custom_call" | custom-call | flops 419430400 | bytes 1 | tf_op jit(solution)/shard_map/weights_2/pallas_call | solution.py:407
  (109 shorter events, 21.1 us)
Async XLA Ops:
  7.2 123.4 %all-gather.3.cloned.1.call-start = ((), (), s32[]{:S(2)}) async-start(), calls=%async_computation | async-start | bytes 2027520 | tf_op jit(solution)/shard_map/all_gather | solution.py:575
  7.2 4.3 %collective-permute-start.3 = (bf16[320,320]{1,0:T(8,128)(2,1)}, bf16[320,320]{1,0:T(8,128)(2,1)S(1)}, u32[]{:S(2)}, u32[]{:S(2)}) collective-permute-start(bf16[320,320]{1,0:T(8,128)(2,1)} %bitcast.57), channel_id=1, source_target_pairs={{0,4},{4,0},{8,12},{12,8},{16,20},{20,16},{24,28},{28,24},{1,5},{5... | collective-permute-start | bytes 614408 | tf_op jit(solution)/shard_map/ppermute | solution.py:449
  7.3 4.2 %collective-permute-start = (bf16[320,1280]{1,0:T(8,128)(2,1)}, bf16[320,1280]{1,0:T(8,128)(2,1)S(1)}, u32[]{:S(2)}, u32[]{:S(2)}) collective-permute-start(bf16[320,1280]{1,0:T(8,128)(2,1)} %bitcast.27), channel_id=1, source_target_pairs={{0,4},{4,0},{8,12},{12,8},{16,20},{20,16},{24,28},{28,24},{1,5},{5... | collective-permute-start | bytes 2457608 | tf_op jit(solution)/shard_map/ppermute | solution.py:449
  7.8 3.7 %collective-permute-start.1 = (bf16[320,1280]{1,0:T(8,128)(2,1)}, bf16[320,1280]{1,0:T(8,128)(2,1)S(1)}, u32[]{:S(2)}, u32[]{:S(2)}) collective-permute-start(bf16[320,1280]{1,0:T(8,128)(2,1)} %bitcast.40), channel_id=1, source_target_pairs={{0,4},{4,0},{8,12},{12,8},{16,20},{20,16},{24,28},{28,24},{1,5},{5... | collective-permute-start | bytes 2457608 | tf_op jit(solution)/shard_map/ppermute | solution.py:449
  10.1 1.4 collective-permute-start.2
  13.0 7.4 %collective-permute-start.4 = (bf16[256,320]{1,0:T(8,128)(2,1)}, bf16[256,320]{1,0:T(8,128)(2,1)S(1)}, u32[]{:S(2)}, u32[]{:S(2)}) collective-permute-start(bf16[256,320]{1,0:T(8,128)(2,1)} %get-tuple-element.72), channel_id=1, source_target_pairs={{0,8},{4,12},{8,0},{12,4},{16,24},{20,28},{24,16},{28,20},{1,9},{5... | collective-permute-start | bytes 491528 | tf_op jit(solution)/shard_map/ppermute | solution.py:455
  21.1 12.6 %copy-start.26 = (bf16[256,320]{1,0:T(8,128)(2,1)S(1)}, bf16[256,320]{1,0:T(8,128)(2,1)}, u32[]{:S(2)}) copy-start(bf16[256,320]{1,0:T(8,128)(2,1)} %get-tuple-element.72) | copy-start | bytes 491524
  21.1 13.3 %copy-start.27 = (bf16[256,320]{1,0:T(8,128)(2,1)S(1)}, bf16[256,320]{1,0:T(8,128)(2,1)}, u32[]{:S(2)}) copy-start(bf16[256,320]{1,0:T(8,128)(2,1)} %get-tuple-element.86) | copy-start | bytes 491524
  21.3 16.1 %collective-permute-start.5 = (bf16[256,320]{1,0:T(8,128)(2,1)}, bf16[256,320]{1,0:T(8,128)(2,1)S(1)}, u32[]{:S(2)}, u32[]{:S(2)}) collective-permute-start(bf16[256,320]{1,0:T(8,128)(2,1)} %get-tuple-element.78), channel_id=1, source_target_pairs={{8,16},{12,20},{16,8},{20,12},{9,17},{13,21},{17,9},{21,13},{10,18... | collective-permute-start | bytes 491528 | tf_op jit(solution)/shard_map/ppermute | solution.py:461
  31.8 9.2 %collective-permute-start.6 = (bf16[256,320]{1,0:T(8,128)(2,1)}, bf16[256,320]{1,0:T(8,128)(2,1)S(1)}, u32[]{:S(2)}, u32[]{:S(2)}) collective-permute-start(bf16[256,320]{1,0:T(8,128)(2,1)} %get-tuple-element.79), channel_id=1, source_target_pairs={{8,16},{12,20},{16,8},{20,12},{9,17},{13,21},{17,9},{21,13},{10,18... | collective-permute-start | bytes 491528 | tf_op jit(solution)/shard_map/ppermute | solution.py:461
  33.7 13.4 %collective-permute-start.8 = (bf16[256,320]{1,0:T(8,128)(2,1)S(1)}, bf16[256,320]{1,0:T(8,128)(2,1)S(1)}, u32[]{:S(2)}, u32[]{:S(2)}) collective-permute-start(bf16[256,320]{1,0:T(8,128)(2,1)S(1)} %copy-done.26), channel_id=1, source_target_pairs={{0,24},{4,28},{24,0},{28,4},{1,25},{5,29},{25,1},{29,5},{2,26},{6,... | collective-permute-start | bytes 491528 | tf_op jit(solution)/shard_map/ppermute | solution.py:461
  34.4 12.7 %collective-permute-start.9 = (bf16[256,320]{1,0:T(8,128)(2,1)S(1)}, bf16[256,320]{1,0:T(8,128)(2,1)S(1)}, u32[]{:S(2)}, u32[]{:S(2)}) collective-permute-start(bf16[256,320]{1,0:T(8,128)(2,1)S(1)} %copy-done.27), channel_id=1, source_target_pairs={{0,24},{4,28},{24,0},{28,4},{1,25},{5,29},{25,1},{29,5},{2,26},{6,... | collective-permute-start | bytes 491528 | tf_op jit(solution)/shard_map/ppermute | solution.py:461
  47.1 5.9 %collective-permute-start.7 = (bf16[256,320]{1,0:T(8,128)(2,1)}, bf16[256,320]{1,0:T(8,128)(2,1)S(1)}, u32[]{:S(2)}, u32[]{:S(2)}) collective-permute-start(bf16[256,320]{1,0:T(8,128)(2,1)} %get-tuple-element.85), channel_id=1, source_target_pairs={{0,8},{4,12},{8,0},{12,4},{16,24},{20,28},{24,16},{28,20},{1,9},{5... | collective-permute-start | bytes 491528 | tf_op jit(solution)/shard_map/ppermute | solution.py:455
  54.4 15.9 %copy-start.7 = (bf16[256,320]{1,0:T(8,128)(2,1)S(1)}, bf16[256,320]{1,0:T(8,128)(2,1)}, u32[]{:S(2)}) copy-start(bf16[256,320]{1,0:T(8,128)(2,1)} %get-tuple-element.102) | copy-start | bytes 491524
  54.8 1.4 collective-permute-start.11
  57.2 18.2 %collective-permute-start.10 = (bf16[256,320]{1,0:T(8,128)(2,1)S(1)}, bf16[256,320]{1,0:T(8,128)(2,1)S(1)}, u32[]{:S(2)}, u32[]{:S(2)}) collective-permute-start(bf16[256,320]{1,0:T(8,128)(2,1)S(1)} %copy-done.28), channel_id=1, source_target_pairs={{0,8},{4,12},{8,0},{12,4},{16,24},{20,28},{24,16},{28,20},{1,9},{5... | collective-permute-start | bytes 491528 | tf_op jit(solution)/shard_map/ppermute | solution.py:455
  70.3 5.2 %collective-permute-start.12 = (bf16[256,320]{1,0:T(8,128)(2,1)S(1)}, bf16[256,320]{1,0:T(8,128)(2,1)S(1)}, u32[]{:S(2)}, u32[]{:S(2)}) collective-permute-start(bf16[256,320]{1,0:T(8,128)(2,1)S(1)} %copy-done.7), channel_id=1, source_target_pairs={{0,4},{4,0},{8,12},{12,8},{16,20},{20,16},{24,28},{28,24},{1,5},{5... | collective-permute-start | bytes 491528 | tf_op jit(solution)/shard_map/ppermute | solution.py:449
  70.3 11.2 %collective-permute-start.13 = (bf16[256,320]{1,0:T(8,128)(2,1)}, bf16[256,320]{1,0:T(8,128)(2,1)S(1)}, u32[]{:S(2)}, u32[]{:S(2)}) collective-permute-start(bf16[256,320]{1,0:T(8,128)(2,1)} %get-tuple-element.107), channel_id=1, source_target_pairs={{24,8},{28,12},{8,24},{12,28},{25,9},{29,13},{9,25},{13,29},{26,10... | collective-permute-start | bytes 491528 | tf_op jit(solution)/shard_map/ppermute | solution.py:461
  70.9 10.5 %collective-permute-start.14 = (bf16[256,320]{1,0:T(8,128)(2,1)}, bf16[256,320]{1,0:T(8,128)(2,1)S(1)}, u32[]{:S(2)}, u32[]{:S(2)}) collective-permute-start(bf16[256,320]{1,0:T(8,128)(2,1)} %get-tuple-element.100), channel_id=1, source_target_pairs={{24,0},{28,4},{0,24},{4,28},{25,1},{29,5},{1,25},{5,29},{26,2},{30... | collective-permute-start | bytes 491528 | tf_op jit(solution)/shard_map/ppermute | solution.py:461
  81.5 13.7 %copy-start.20 = (bf16[256,320]{1,0:T(8,128)(2,1)}, bf16[256,320]{1,0:T(8,128)(2,1)S(1)}, u32[]{:S(2)}) copy-start(bf16[256,320]{1,0:T(8,128)(2,1)S(1)} %collective-permute-done.13.refs_5_) | copy-start | bytes 491524
  81.5 14.6 %copy-start.19 = (bf16[256,320]{1,0:T(8,128)(2,1)}, bf16[256,320]{1,0:T(8,128)(2,1)S(1)}, u32[]{:S(2)}) copy-start(bf16[256,320]{1,0:T(8,128)(2,1)S(1)} %collective-permute-done.14.refs_4_) | copy-start | bytes 491524
  81.5 10.6 %collective-permute-start.15 = (bf16[256,320]{1,0:T(8,128)(2,1)}, bf16[256,320]{1,0:T(8,128)(2,1)S(1)}, u32[]{:S(2)}, u32[]{:S(2)}) collective-permute-start(bf16[256,320]{1,0:T(8,128)(2,1)} %get-tuple-element.108), channel_id=1, source_target_pairs={{16,8},{20,12},{8,16},{12,20},{17,9},{21,13},{9,17},{13,21},{18,10... | collective-permute-start | bytes 491528 | tf_op jit(solution)/shard_map/ppermute | solution.py:461
  85.0 10.2 %collective-permute-start.16 = (bf16[256,320]{1,0:T(8,128)(2,1)}, bf16[256,320]{1,0:T(8,128)(2,1)S(1)}, u32[]{:S(2)}, u32[]{:S(2)}) collective-permute-start(bf16[256,320]{1,0:T(8,128)(2,1)} %get-tuple-element.112), channel_id=1, source_target_pairs={{16,8},{20,12},{8,16},{12,20},{17,9},{21,13},{9,17},{13,21},{18,10... | collective-permute-start | bytes 491528 | tf_op jit(solution)/shard_map/ppermute | solution.py:461
  96.0 22.4 %copy-start.25 = (bf16[256,320]{1,0:T(8,128)(2,1)S(1)}, bf16[256,320]{1,0:T(8,128)(2,1)}, u32[]{:S(2)}) copy-start(bf16[256,320]{1,0:T(8,128)(2,1)} %get-tuple-element.115) | copy-start | bytes 491524
  99.6 1.6 collective-permute-start.18
  102.2 11.7 %collective-permute-start.19 = (bf16[320,320]{1,0:T(8,128)(2,1)S(1)}, bf16[320,320]{1,0:T(8,128)(2,1)S(1)}, u32[]{:S(2)}, u32[]{:S(2)}) collective-permute-start(bf16[320,320]{1,0:T(8,128)(2,1)S(1)} %fusion), channel_id=1, source_target_pairs={{16,17},{17,16},{18,19},{19,18},{20,21},{21,20},{22,23},{23,22},{2... | collective-permute-start | bytes 614408 | tf_op jit(solution)/shard_map/ppermute | solution.py:469
  114.0 15.7 %collective-permute-start.20 = (bf16[320,320]{1,0:T(8,128)(2,1)S(1)}, bf16[320,320]{1,0:T(8,128)(2,1)S(1)}, u32[]{:S(2)}, u32[]{:S(2)}) collective-permute-start(bf16[320,320]{1,0:T(8,128)(2,1)S(1)} %add_convert_fusion.1), channel_id=1, source_target_pairs={{16,18},{17,19},{18,16},{19,17},{20,22},{21,23},{22,20},{23,21},{2... | collective-permute-start | bytes 614408 | tf_op jit(solution)/shard_map/ppermute | solution.py:469
  118.4 12.1 %collective-permute-start.17 = (bf16[256,320]{1,0:T(8,128)(2,1)S(1)}, bf16[256,320]{1,0:T(8,128)(2,1)S(1)}, u32[]{:S(2)}, u32[]{:S(2)}) collective-permute-start(bf16[256,320]{1,0:T(8,128)(2,1)S(1)} %copy-done.25), channel_id=1, source_target_pairs={{0,8},{4,12},{8,0},{12,4},{16,24},{20,28},{24,16},{28,20},{1,9},{5... | collective-permute-start | bytes 491528 | tf_op jit(solution)/shard_map/ppermute | solution.py:455
  131.5 1.7 collective-permute-start.21
  133.2 11.2 %collective-permute-start.22 = (bf16[512,320]{1,0:T(8,128)(2,1)S(1)}, bf16[512,320]{1,0:T(8,128)(2,1)S(1)}, u32[]{:S(2)}, u32[]{:S(2)}) collective-permute-start(bf16[512,320]{1,0:T(8,128)(2,1)S(1)} %constant_dynamic-update-slice_fusion.refs_1_), channel_id=1, source_target_pairs={{0,1},{1,0},{2,3},{3,2},{4,5},{5,4},{6,7},{7,6},{8,9},{9,8},{10,11... | collective-permute-start | bytes 983048 | tf_op jit(solution)/shard_map/ppermute | solution.py:469
  133.4 21.2 %collective-permute-start.24 = (bf16[512,320]{1,0:T(8,128)(2,1)S(1)}, bf16[512,320]{1,0:T(8,128)(2,1)S(1)}, u32[]{:S(2)}, u32[]{:S(2)}) collective-permute-start(bf16[512,320]{1,0:T(8,128)(2,1)S(1)} %constant_dynamic-update-slice_fusion.refs_1_), channel_id=1, source_target_pairs={{0,3},{1,2},{2,1},{3,0},{4,7},{5,6},{6,5},{7,4},{8,11},{9,10},{10,... | collective-permute-start | bytes 983048 | tf_op jit(solution)/shard_map/ppermute | solution.py:469
  136.3 34.9 %collective-permute-start.23 = (bf16[512,320]{1,0:T(8,128)(2,1)S(1)}, bf16[512,320]{1,0:T(8,128)(2,1)S(1)}, u32[]{:S(2)}, u32[]{:S(2)}) collective-permute-start(bf16[512,320]{1,0:T(8,128)(2,1)S(1)} %constant_dynamic-update-slice_fusion.refs_1_), channel_id=1, source_target_pairs={{0,2},{1,3},{2,0},{3,1},{4,6},{5,7},{6,4},{7,5},{8,10},{9,11},{10,... | collective-permute-start | bytes 983048 | tf_op jit(solution)/shard_map/ppermute | solution.py:469
  (23 other events, 45.4 us)
Sparse Core Ops, SparseCore 0:
  57.3 52.1 all-gather.2

commit v2 on v1

--- a/solution.py
+++ b/solution.py
@@ -138,10 +138,10 @@
 
 
 def forward_kernel(which, upper, first_stage, n_alias, *refs):
-    x, skip_a, skip_b = refs[:3]
-    own, other = refs[3:7], refs[7:11]
-    refs = refs[11 + n_alias :]
-    hop, rows_keep, rows_send, out_a, out_keep, out_send, slopes = refs[:7]
+    x, skips = refs[:2]
+    own, other = refs[2:6], refs[6:10]
+    refs = refs[10 + n_alias :]
+    hop, rows_keep, rows_send, pair, out_keep, out_send, slopes = refs[:7]
     x_here, rows_here, outs_here, slopes_here, skips_here, first_here, second_here, code_here, merge_here = refs[7:16]
     sized, semaphores = refs[16:]
     groups = sized.shape[0]
@@ -151,7 +151,7 @@
     def _():
         copies = Copies(semaphores, core)
         if upper:
-            skip_copies = [copies.start(skip_a, skips_here.at[0])]
+            skip_copies = [copies.start(skips.at[1], skips_here.at[0])]
         if not (upper and first_stage):
             x_copy = take_rows(copies, x, x_here)
         merge_copies, weight_copies = [], []
@@ -166,7 +166,7 @@
                 ]
             )
             if upper and at == 0:
-                skip_copies.append(copies.start(skip_b, skips_here.at[1]))
+                skip_copies.append(copies.start(skips.at[0], skips_here.at[1]))
         finals = []
         for at in (0, 1):
             if at == 0:
@@ -194,7 +194,10 @@
 
             result = layer_forward(merged, first_here.at[at], second_here.at[at], code_of, slopes_here.at[at])
             outs_here[at] = result
-            finals.append(copies.start(outs_here.at[at], (out_a, hop)[at]))
+            if not upper:
+                finals.append(copies.start(outs_here.at[at], pair.at[at]))
+            if at == 1:
+                finals.append(copies.start(outs_here.at[at], hop))
             finals.append(copies.start_layer_out(at, outs_here.at[at], out_keep, out_send))
             finals.append(copies.start(slopes_here.at[at], slopes.at[at]))
             arrived = result
@@ -208,7 +211,7 @@
     refs = refs[12 + n_alias :]
     hop, kept, sent = refs[:3]
     if upper:
-        grads, back_b = refs[3:5]
+        grads, pair = refs[3:5]
         refs = refs[5:]
     else:
         refs = refs[3:]
@@ -219,7 +222,8 @@
     @pl.when(stage == which)
     def _():
         copies = Copies(semaphores, core)
-        arrived_copy = take_rows(copies, arrived, arrived_here)
+        first_low = not upper and len(arrived.shape) == 3
+        arrived_copy = take_rows(copies, arrived.at[0] if first_low else arrived, arrived_here)
         layers = (1,) if which == 0 else (1, 0)
         waits = {}
         for at in layers:
@@ -232,7 +236,7 @@
             if middle:
                 waits[at].append(copies.start_layer(at, own[2], other[2], merge_here.at[at]))
             elif not upper and at == 1:
-                extra_copies = [copies.start(extra_a, extra_here.at[0])]
+                extra_copies = [copies.start(arrived.at[1] if first_low else extra_a, extra_here.at[0])]
                 if which > 0:
                     extra_copies.append(copies.start(extra_b, extra_here.at[1]))
         arrived_copy.wait()
@@ -255,12 +259,8 @@
                 finals.append(copies.start(grads_here.at[at], grads.at[at]))
                 if middle:
                     returned = nt(grad, merge_here[at]).astype(BF16)
-                    if at == 1:
-                        grads_here[3] = returned
-                        finals.append(copies.start(grads_here.at[3], back_b))
-                    else:
-                        grads_here[4] = added(grad, returned)
-                        finals.append(copies.start(grads_here.at[4], hop))
+                    grads_here[3 + at] = returned if at == 1 else added(grad, returned)
+                    finals.append(copies.start(grads_here.at[3 + at], pair.at[at]))
                 out_grad = grad
             elif at == 1:
                 extra_copies[0].wait()
@@ -276,23 +276,24 @@
 
 
 def returns_kernel(which, middle, n_alias, *refs):
-    grads, skip_a, skip_b, own, other = refs[:5]
-    merges, back_a, back_b, grads_here, skips_here, merge_here, merges_here, semaphores = refs[5 + n_alias :]
+    grads, skips, own, other = refs[:4]
+    keep, send, back_a, back_b, grads_here, skips_here, merge_here, merges_here, semaphores = refs[4 + n_alias :]
     stage, core = place()
 
     @pl.when(stage == which)
     def _():
         copies = Copies(semaphores, core)
         waits = [copies.start(grads, grads_here)]
-        for at, skip in ((0, skip_a), (1, skip_b)):
-            waits.append(copies.start(skip, skips_here.at[at]))
+        for at in (0, 1):
+            waits.append(copies.start(skips.at[1 - at], skips_here.at[at]))
             waits.append(copies.start_layer(at, own, other, merge_here.at[at]))
         for copy in waits:
             copy.wait()
         finals = []
         for at in (0, 1):
             merges_here[jnp.where(core == at, 1, 0)] = tn(skips_here[at], grads_here[at]).astype(BF16)
-        finals.append(copies.start(merges_here, merges))
+        finals.append(copies.start(merges_here.at[1], keep))
+        finals.append(copies.start(merges_here.at[0], send))
         if not middle:
             for at, back in ((0, back_a), (1, back_b)):
                 skips_here[at] = nt(grads_here[at], merge_here[at]).astype(BF16)
@@ -341,40 +342,55 @@
     out_grad = grads_here[...]
     finals = []
 
+    def by_core(mine, rest):
+        return jnp.concatenate([jnp.where(core == 0, mine, rest), jnp.where(core == 0, rest, mine)], axis=0)
+
     def column_part(cols, value):
         both = nn(table, clock_here[:, cols])
-        own_code = jnp.where(core == 0, both[:groups], both[groups : 2 * groups])
-        rest = jnp.where(core == 0, both[groups : 2 * groups], both[:groups])
-        pre = add_rows(nn(normed, first_here[:, cols]), jnp.concatenate([own_code, rest], axis=0))
+        code_rows = by_core(both[:groups], both[groups : 2 * groups])
+        pre = add_rows(nn(normed, first_here[:, cols]), code_rows)
         hidden, slope = gelu_parts(pre)
+        hidden = hidden.astype(BF16)
         pre_grad = (nn(out_grad, second_here[:, cols]) * slope).astype(BF16)
         wide_grad = pre_grad.astype(F32)
         lines = [jnp.sum(wide_grad[i * tall : (i + 1) * tall], axis=0, keepdims=True) for i in range(2 * groups)]
-        sums_here[slot, pl.ds(0, 2 * groups), cols] = jnp.concatenate(lines, axis=0)
-        for kind, value in ((0, tn(normed, pre_grad)), (1, tn(out_grad, hidden.astype(BF16)))):
+        lines = by_core(jnp.concatenate(lines[:groups], axis=0), jnp.concatenate(lines[groups:], axis=0))
+        lines = jnp.concatenate([lines, jnp.zeros((PAD - 2 * groups, lines.shape[1]), F32)], axis=0)
+        sums_here[slot, :, cols] = lines
+        for kind, right in ((0, pre_grad), (1, hidden)):
+            value = tn((normed, out_grad)[kind], right)
             if cols.start == 0 and kind == 0:
                 for copy in total_copies:
                     copy.wait()
             for i in range(n_before):
                 value = value + before_here[i, kind, :, cols]
             results_here[kind, :, cols] = value
+            target = (out_first, out_second)[kind] if last else totals.at[kind]
+            finals.append(copies.start(results_here.at[kind, :, cols], target.at[:, cols]))
 
     over_columns(results_here.shape[2], WEIGHT_PARTS, None, column_part)
-    if not last:
-        finals = [copies.start(results_here, totals), copies.start(sums_here, sums), copies.start(codes_here, codes)]
+    if last:
+        flat = (sums_here.shape[0] * PAD, -1)
+        codes_flat = codes_here[...].reshape(flat[0], codes_here.shape[2])
+        sums_flat = sums_here[...].astype(BF16).reshape(flat[0], sums_here.shape[2])
+        before_here[0, 0] = tn(codes_flat, sums_flat)
+        finals.append(copies.start(before_here.at[0, 0], out_clock))
     else:
-        finals = [copies.start(results_here.at[0], out_first), copies.start(results_here.at[1], out_second)]
-        total = jnp.zeros(out_clock.shape, F32)
-        for replica in range(sums_here.shape[0]):
-            table = codes_here[replica]
-            mine = jnp.where(core == 0, table[:groups], table[groups : 2 * groups])
-            rest = jnp.where(core == 0, table[groups : 2 * groups], table[:groups])
-            order = jnp.concatenate([mine, rest], axis=0)
-            total = total + tn(order, sums_here[replica, pl.ds(0, 2 * groups), :].astype(BF16))
-        before_here[0, 0] = total
-        finals.append(copies.start(before_here.at[0, 0], out_clock))
+        finals += [copies.start(sums_here, sums), copies.start(codes_here, codes)]
     for copy in finals:
         copy.wait()
+
+
+def add_kernel(half, a, b, out, here, semaphores):
+    stage, core = place()
+
+    @pl.when(stage >= half)
+    def _():
+        copies = Copies(semaphores, core)
+        for copy in [copies.start(a, here.at[0]), copies.start(b, here.at[1])]:
+            copy.wait()
+        here[2] = added(here[0], here[1])
+        copies.start(here.at[2], out).wait()
 
 
 def assemble_kernel(turns, n_alias, *refs):
@@ -492,21 +508,21 @@
 
     def forward(stage, x, skips):
         upper, first_stage = stage >= half, stage in (0, half)
-        args = [x, *(skips or (table, table))]
+        args = [x, x if skips is None else skips]
         args += [w_first, w_second, code, w_merge, other_first, other_second, other_code, other_merge]
-        keys = ("keep", "send", ("a", stage), "out_keep", "out_send", "slopes")
+        keys = ("keep", "send", ("pair", stage), "out_keep", "out_send", "slopes")
         aliases = {}
         for output, key in enumerate(keys):
             if key in saved:
                 aliases[len(args)] = 1 + output
                 args.append(saved[key])
-        scratch = [pltpu.VMEM(native if x.ndim == 3 else block, BF16), pltpu.VMEM(two_blocks, BF16)]
+        scratch = [pltpu.VMEM(native if stage == 0 else block, BF16), pltpu.VMEM(two_blocks, BF16)]
         scratch += [pltpu.VMEM(two_blocks, BF16), pltpu.VMEM(slopes, BF16), pltpu.VMEM(two_blocks, BF16)]
         scratch += two_weights + [pltpu.VMEM((2, PAD, hidden), F32), pltpu.VMEM(merge_pair, BF16)]
         scratch += [group_marker, pltpu.SemaphoreType.DMA((24,))]
         result = call(
             functools.partial(forward_kernel, stage, upper, first_stage, len(aliases)),
-            args, [shape(block)] * 6 + [shape(slopes)], scratch, aliases, flops, f"forward_stage_{stage}",
+            args, [shape(block)] * 3 + [shape(two_blocks)] + [shape(block)] * 2 + [shape(slopes)], scratch, aliases, flops, f"forward_stage_{stage}",
         )
         saved.update(zip(keys, result[1:]))
         return result[0]
@@ -519,33 +535,33 @@
             x = hop_between(sent, stage)
         if stage < half:
             up = stages - 1 - stage
-            skips[up] = (between(sent, stage, up), between(saved["a", stage], stage, up))
+            skips[up] = between(saved["pair", stage], stage, up)
             if stage == half - 1:
-                x = skips[up][0]
+                x = skips[up]
 
     weights_of = [w_first, w_second, w_merge, other_first, other_second, other_merge]
     back_pairs = {}
     arrived = cotangent.transpose(0, 2, 1)
     kept = []
-    merges = None
-
-    def backward_scratch():
-        scratch = [pltpu.VMEM(native if arrived.ndim == 3 else block, BF16), pltpu.VMEM(two_blocks, BF16)]
+    merges = []
+
+    def backward_scratch(arrived_shape=block):
+        scratch = [pltpu.VMEM(arrived_shape, BF16), pltpu.VMEM(two_blocks, BF16)]
         scratch += [pltpu.VMEM(slopes, BF16), pltpu.VMEM(two_blocks, BF16)]
         scratch += [pltpu.VMEM((5,) + block, BF16)] + two_weights
         scratch += [pltpu.VMEM(merge_pair, BF16), pltpu.SemaphoreType.DMA((24,))]
         return scratch
 
     def returns(stage, grads, waited):
-        args = [after(grads, waited), *skips[stage], w_merge, other_merge]
+        args = [after(grads, waited), skips[stage], w_merge, other_merge]
         aliases = {}
-        if merges is not None:
-            aliases = {len(args): 0}
-            args.append(merges)
+        if merges:
+            aliases = {len(args): 0, len(args) + 1: 1}
+            args += merges
         scratch = [pltpu.VMEM(two_blocks, BF16)] * 2 + [pltpu.VMEM(merge_pair, BF16)] * 2
         return call(
             functools.partial(returns_kernel, stage, stage == half, len(aliases)),
-            args, [shape(merge_pair), shape(block), shape(block)], scratch + [pltpu.SemaphoreType.DMA((12,))],
+            args, [shape((width, width))] * 2 + [shape(block), shape(block)], scratch + [pltpu.SemaphoreType.DMA((12,))],
             aliases, flops // 4, f"returns_stage_{stage}",
         )
 
@@ -554,20 +570,21 @@
         args = [arrived, saved["keep"], saved["send"], saved["slopes"], arrived, arrived] + weights_of
         aliases = {len(args) + i: 1 + i for i in range(len(kept))}
         args += kept
-        sent, *kept, grads, back_b = call(
+        sent, *kept, grads, pair = call(
             functools.partial(backward_kernel, stage, True, middle, len(aliases)),
-            args, [shape(block)] * 3 + [shape(two_blocks), shape(block)], backward_scratch(),
+            args, [shape(block)] * 3 + [shape(two_blocks)] * 2,
+            backward_scratch(native if stage == stages - 1 else block),
             aliases, flops, f"backward_stage_{stage}",
         )
         low = stages - 1 - stage
         if middle:
-            sent = after(sent, *[value for pair in back_pairs.values() for value in pair])
-            arrived = between(sent, half, half - 1)
-            back_pairs[low] = (None, between(after(back_b, sent), half, half - 1))
+            pair = after(pair, *[value for values in back_pairs.values() for value in values])
+            arrived = between(pair, half, half - 1)
+            back_pairs[low] = (None, arrived)
             middle_grads = grads
         else:
             arrived = hop_between(sent, stage - 1)
-            merges, back_a, back_b = returns(stage, grads, sent)
+            *merges, back_a, back_b = returns(stage, grads, sent)
             back_pairs[low] = (between(back_a, stage, low + 1), between(back_b, stage, low))
             if stage == stages - 1:
                 came = swap_cores(after(saved["send"], back_b))
@@ -587,14 +604,20 @@
 
     outputs = assemble([(0, 0), (half, stages - 1)], None, sent)
 
-    def merge_gradients():
-        total = (merges[1].astype(F32) + swap_cores(merges[0]).astype(F32)).astype(BF16)
+    def add(a, b):
+        return call(
+            functools.partial(add_kernel, half), [a, b], [shape((width, width))],
+            [pltpu.VMEM((3, width, width), BF16), pltpu.SemaphoreType.DMA((4,))], None, 0, "add_merges",
+        )[0]
+
+    def merge_gradients(waited):
+        keep, send = returns(half, after(middle_grads, *waited), waited[0])[:2]
+        total = add(keep, swap_cores(send))
         distance = 1
         while distance < replicas:
-            came = over_replicas(total, distance, high_stages)
-            total = (total.astype(F32) + came.astype(F32)).astype(BF16)
+            total = add(total, over_replicas(total, distance, high_stages))
             distance *= 2
-        return jnp.where(rank // 2 < half, 0.0, total.astype(F32))
+        return total
 
     for stage in range(half - 1, -1, -1):
         extra_b = back_pairs[stage - 1][0] if stage > 0 else arrived
@@ -608,9 +631,7 @@
         if stage > 0:
             arrived = hop_between(sent, stage - 1)
         if stage == 1:
-            merges = returns(half, middle_grads, sent)[0]
-            grad_merge = merge_gradients()
-            arrived = after(arrived, grad_merge, gathered)
+            arrived = after(arrived, gathered)
 
     kept_grad, sent_grad = kept
     came_grad = swap_cores(sent_grad)
@@ -628,7 +649,7 @@
         scratch = [pltpu.VMEM((2 * rows + PAD, width), BF16), pltpu.VMEM((2 * rows, width), BF16)]
         scratch += [pltpu.VMEM((width, hidden), BF16)] * 3
         scratch += [pltpu.VMEM((max(1, len(before)),) + matrices, F32), pltpu.VMEM(matrices, F32)]
-        scratch += [pltpu.VMEM(lines, F32), pltpu.VMEM(codes, BF16), pltpu.SemaphoreType.DMA((16,))]
+        scratch += [pltpu.VMEM(lines, F32), pltpu.VMEM(codes, BF16), pltpu.SemaphoreType.DMA((32,))]
         return call(
             functools.partial(weight_kernel, d, groups, len(before), last),
             args, outs, scratch, None, weight_flops, f"weights_{d}",
@@ -650,6 +671,8 @@
             sums = tuple(result[1:])
     grad_first, grad_second, grad_clock = result
 
+    total = merge_gradients((grads[distances[-1]], sums[0]))
+    grad_merge = jnp.where(rank // 2 < half, 0.0, total.astype(F32))
     return (
         outputs.transpose(0, 2, 1)[None],
         grad_first[None],

time: 189 us -> 197 us (1.042)
  waiting for transfers between devices: 58.8 us -> 74.2 us
  starting transfers between devices: 51 us -> 41.1 us
  Pallas kernels: 48.4 us -> 51.2 us
    all_gather x1, waiting for transfers between devices: 0.01 us -> 7.48 us  [local(): gathered = lax.all_gather(packed, 'dp')]
    ppermute x4, waiting for transfers between devices: 15.6 us -> 21.6 us  [hop_between(): lax.ppermute(block, 'section', [(2 * a + c, 2 * b + c) for a, b in pairs....]
    ppermute x8 -> x5, waiting for transfers between devices: 10.8 us -> 16.6 us  [between(): lax.ppermute(block, 'section', [(2 * i + c, 2 * j + c) for i, j in pairs...]
    ppermute x8 -> x5, starting transfers between devices: 21.8 us -> 16 us  [between(): lax.ppermute(block, 'section', [(2 * i + c, 2 * j + c) for i, j in pairs...]
    ppermute x5, waiting for transfers between devices: 28.6 us -> 23.7 us  [over_replicas(): return lax.ppermute(block, ('section', 'dp'), route)]
    ppermute x5, starting transfers between devices: 13.2 us -> 8.72 us  [over_replicas(): return lax.ppermute(block, ('section', 'dp'), route)]
    pallas_call x16 -> x19, Pallas kernels: 48.4 us -> 51.2 us  [call(): pl.pallas_call(kernel, out_shape=outs, in_specs=[IN_HBM] * len(args), out...]
    unnamed x59 -> x55, local copies, waits for them, and re-layouts: 8.77 us -> 9.67 us
  transfers between devices with their start and end apart: 26 -> 23, of which waited for: 16 -> 16; matrix products, arithmetic and copies ran while one was open for 4% -> 2% of each run, Pallas kernels for 20% -> 21%
where the time goes in v2:
time: 197 us; the launch traced here: 196 us
  waiting for transfers between devices  74.2 us (38%)
  Pallas kernels  51.2 us (26%)
  starting transfers between devices  41.1 us (21%)
  between operations  14.5 us (7%)
  local copies, waits for them, and re-layouts  9.79 us (5%)
  other arithmetic  4.12 us (2%)
    pallas_call x19, Pallas kernels, call(): pl.pallas_call(kernel, out_shape=outs, in_specs=[IN_HBM] * len(args), out...  51.2 us
    ppermute x5, waiting for transfers between devices, over_replicas(): return lax.ppermute(block, ('section', 'dp'), route)  23.7 us
    ppermute x4, waiting for transfers between devices, hop_between(): lax.ppermute(block, 'section', [(2 * a + c, 2 * b + c) for a, b in pairs....  21.6 us
    ppermute x5, waiting for transfers between devices, between(): lax.ppermute(block, 'section', [(2 * i + c, 2 * j + c) for i, j in pairs...  16.6 us
    ppermute x5, starting transfers between devices, between(): lax.ppermute(block, 'section', [(2 * i + c, 2 * j + c) for i, j in pairs...  16 us
    ppermute x4, starting transfers between devices, hop_between(): lax.ppermute(block, 'section', [(2 * a + c, 2 * b + c) for a, b in pairs....  15 us
    unnamed x55, local copies, waits for them, and re-layouts  9.67 us
    ppermute x5, starting transfers between devices, over_replicas(): return lax.ppermute(block, ('section', 'dp'), route)  8.72 us
  transfers between devices with their start and end apart: 23, of which 16 were waited for; matrix products, arithmetic and copies ran while one was open for 2% of the time, Pallas kernels for 21%

profile of v2, /device:TPU:4, one launch (start us, length us, event | category | flops | bytes accessed | tf_op | source)
XLA Modules:
  0.0 196.3 jit_solution(6769858118135376368)
XLA Ops:
  8.7 1.4 fusion.5.refs_4_
  13.0 1.6 collective-permute-start.4
  14.5 5.9 %collective-permute-done.4.refs_0_.refs_1_ = bf16[256,320]{1,0:T(8,128)(2,1)S(1)} collective-permute-done((bf16[256,320]{1,0:T(8,128)(2,1)}, bf16[256,320]{1,0:T(8,128)(2,1)S(1)}, u32[]{:S(2)}, u32[]{:S(2)}) %collective-permute-start.4) | collective-permute-done | bytes 163872 | tf_op jit(solution)/shard_map/ppermute | solution.py:471
  21.3 10.6 %collective-permute-start.5 = (bf16[2,256,320]{2,1,0:T(8,128)(2,1)}, bf16[2,256,320]{2,1,0:T(8,128)(2,1)S(1)}, u32[]{:S(2)}, u32[]{:S(2)}) collective-permute-start(bf16[2,256,320]{2,1,0:T(8,128)(2,1)} %get-tuple-element.77), channel_id=1, source_target_pairs={{8,16},{12,20},{16,8},{20,12},{9,17},{13,21},{17,9},{21,13},{10,18... | collective-permute-start | bytes 983048 | tf_op jit(solution)/shard_map/ppermute | solution.py:477
  32.6 8.4 %collective-permute-done.5.refs_0_.refs_1_ = bf16[2,256,320]{2,1,0:T(8,128)(2,1)S(1)} collective-permute-done((bf16[2,256,320]{2,1,0:T(8,128)(2,1)}, bf16[2,256,320]{2,1,0:T(8,128)(2,1)S(1)}, u32[]{:S(2)}, u32[]{:S(2)}) %collective-permute-start.5) | collective-permute-done | bytes 327712 | tf_op jit(solution)/shard_map/ppermute | solution.py:477
  41.8 5.4 %forward_stage_2.1 = (bf16[256,320]{1,0:T(8,128)(2,1)}, bf16[256,320]{1,0:T(8,128)(2,1)}, bf16[256,320]{1,0:T(8,128)(2,1)}, bf16[2,256,320]{2,1,0:T(8,128)(2,1)}...) custom-call(bf16[2,256,320]{2,1,0:T(8,128)(2,1)} %copy-done.5, ...), custom_call_target="tpu_custom_call", output_to_operand_aliasing={{1}: (10, {}), {2}: (11, {}), {4}: (12, {}), {5}: (13, {}),... | custom-call | bytes 1 | tf_op jit(solution)/shard_map/forward_stage_2/pallas_call | solution.py:423
  47.3 6.0 %collective-permute-done.6.refs_0_ = bf16[256,320]{1,0:T(8,128)(2,1)S(1)} collective-permute-done((bf16[256,320]{1,0:T(8,128)(2,1)}, bf16[256,320]{1,0:T(8,128)(2,1)S(1)}, u32[]{:S(2)}, u32[]{:S(2)}) %collective-permute-start.6) | collective-permute-done | bytes 163872 | tf_op jit(solution)/shard_map/ppermute | solution.py:471
  57.6 13.3 %collective-permute-start.8 = (bf16[256,320]{1,0:T(8,128)(2,1)S(1)}, bf16[256,320]{1,0:T(8,128)(2,1)S(1)}, u32[]{:S(2)}, u32[]{:S(2)}) collective-permute-start(bf16[256,320]{1,0:T(8,128)(2,1)S(1)} %copy-done.26), channel_id=1, source_target_pairs={{0,8},{4,12},{8,0},{12,4},{16,24},{20,28},{24,16},{28,20},{1,9},{5... | collective-permute-start | bytes 491528 | tf_op jit(solution)/shard_map/ppermute | solution.py:471
  72.3 3.8 %collective-permute-done.8.refs_0_.refs_4_.refs_5_ = bf16[256,320]{1,0:T(8,128)(2,1)S(1)} collective-permute-done((bf16[256,320]{1,0:T(8,128)(2,1)S(1)}, bf16[256,320]{1,0:T(8,128)(2,1)S(1)}, u32[]{:S(2)}, u32[]{:S(2)}) %collective-permute-start.8) | collective-permute-done | bytes 163872 | tf_op jit(solution)/shard_map/ppermute | solution.py:471
  76.8 5.3 %backward_stage_2.1 = (bf16[256,320]{1,0:T(8,128)(2,1)}, bf16[256,320]{1,0:T(8,128)(2,1)}, bf16[256,320]{1,0:T(8,128)(2,1)}, bf16[2,256,320]{2,1,0:T(8,128)(2,1)}, bf16[2,256,320]{2,1,0:T(8,128)(2,1)}) custom-call(bf16[256,320]{1,0:T(8,128)(2,1)} %copy-done.7, ...), custom_call_target="tpu_custom_call", output_to_operand_aliasing={{1}: (12, {}), {2}: (13, {})} | custom-call | bytes 1 | tf_op jit(solution)/shard_map/backward_stage_2/pallas_call | solution.py:423
  82.2 3.4 %collective-permute-start.13 = (bf16[2,256,320]{2,1,0:T(8,128)(2,1)}, bf16[2,256,320]{2,1,0:T(8,128)(2,1)S(1)}, u32[]{:S(2)}, u32[]{:S(2)}) collective-permute-start(bf16[2,256,320]{2,1,0:T(8,128)(2,1)} %get-tuple-element.106), channel_id=1, source_target_pairs={{16,8},{20,12},{8,16},{12,20},{17,9},{21,13},{9,17},{13,21},{18,10... | collective-permute-start | bytes 983048 | tf_op jit(solution)/shard_map/ppermute | solution.py:477
  85.6 2.0 outputs_0_2.1.refs_2_
  87.6 8.2 %collective-permute-done.13.refs_0_.refs_4_ = bf16[2,256,320]{2,1,0:T(8,128)(2,1)S(1)} collective-permute-done((bf16[2,256,320]{2,1,0:T(8,128)(2,1)}, bf16[2,256,320]{2,1,0:T(8,128)(2,1)S(1)}, u32[]{:S(2)}, u32[]{:S(2)}) %collective-permute-start.13) | collective-permute-done | bytes 327712 | tf_op jit(solution)/shard_map/ppermute | solution.py:477
  96.9 5.9 %collective-permute-done.14.refs_0_.refs_5_ = bf16[256,320]{1,0:T(8,128)(2,1)S(1)} collective-permute-done((bf16[256,320]{1,0:T(8,128)(2,1)}, bf16[256,320]{1,0:T(8,128)(2,1)S(1)}, u32[]{:S(2)}, u32[]{:S(2)}) %collective-permute-start.14) | collective-permute-done | bytes 163872 | tf_op jit(solution)/shard_map/ppermute | solution.py:471
  102.8 7.5 %all-gather.3.cloned.1.call-done = bf16[2112,320]{1,0:T(8,128)(2,1)} async-done(((bf16[528,320]{1,0:T(8,128)(2,1)}), bf16[2112,320]{1,0:T(8,128)(2,1)}) %all-gather.3.cloned.1.call-update) | async-done | bytes 1351696 | tf_op jit(solution)/shard_map/all_gather | solution.py:592
  112.7 2.3 %collective-permute-start.18 = (bf16[512,320]{1,0:T(8,128)(2,1)S(1)}, bf16[512,320]{1,0:T(8,128)(2,1)S(1)}, u32[]{:S(2)}, u32[]{:S(2)}) collective-permute-start(bf16[512,320]{1,0:T(8,128)(2,1)S(1)} %constant_dynamic-update-slice_fusion.refs_1_), channel_id=1, source_target_pairs={{0,3},{1,2},{2,1},{3,0},{4,7},{5,6},{6,5},{7,4},{8,11},{9,10},{10,... | collective-permute-start | bytes 983048 | tf_op jit(solution)/shard_map/ppermute | solution.py:485
  116.5 6.6 %weights_0.1 = (f32[2,320,1280]{2,1,0:T(8,128)}, f32[4,16,1280]{2,1,0:T(8,128)}, bf16[4,16,320]{2,1,0:T(8,128)(2,1)}) custom-call(bf16[4,528,320]{2,1,0:T(8,128)(2,1)} %bitcast.49, bf16[512,320]{1,0:T(8,128)(2,1)} %copy-done.12, bf16[320,1280]{1,0:T(8,128)(2,1)} %bitcast.32, bf16[320,1280]{1,0:T(8,128)(2,1)} %bitcast.45, bf16[320,1280]{1,0:T(8,128)(2,1)} %bitcast.64, ...), custom_call_target="tpu_custom_call" | custom-call | flops 419430400 | bytes 1 | tf_op jit(solution)/shard_map/weights_0/pallas_call | solution.py:423
  124.3 6.9 %weights_1.1 = (f32[2,320,1280]{2,1,0:T(8,128)}, f32[4,16,1280]{2,1,0:T(8,128)}, bf16[4,16,320]{2,1,0:T(8,128)(2,1)}) custom-call(bf16[4,528,320]{2,1,0:T(8,128)(2,1)} %bitcast.50, bf16[512,320]{1,0:T(8,128)(2,1)} %copy-done.17, bf16[320,1280]{1,0:T(8,128)(2,1)} %bitcast.33, bf16[320,1280]{1,0:T(8,128)(2,1)} %bitcast.46, bf16[320,1280]{1,0:T(8,128)(2,1)} %bitcast.65, ...), custom_call_target="tpu_custom_call" | custom-call | flops 419430400 | bytes 1 | tf_op jit(solution)/shard_map/weights_1/pallas_call | solution.py:423
  131.2 2.3 %collective-permute-done.18.refs_1_ = bf16[512,320]{1,0:T(8,128)(2,1)S(1)} collective-permute-done((bf16[512,320]{1,0:T(8,128)(2,1)S(1)}, bf16[512,320]{1,0:T(8,128)(2,1)S(1)}, u32[]{:S(2)}, u32[]{:S(2)}) %collective-permute-start.18) | collective-permute-done | bytes 327712 | tf_op jit(solution)/shard_map/ppermute | solution.py:485
  134.2 6.7 %weights_3.1 = (f32[2,320,1280]{2,1,0:T(8,128)}, f32[4,16,1280]{2,1,0:T(8,128)}, bf16[4,16,320]{2,1,0:T(8,128)(2,1)}) custom-call(bf16[4,528,320]{2,1,0:T(8,128)(2,1)} %bitcast.51, bf16[512,320]{1,0:T(8,128)(2,1)} %copy-done.18, bf16[320,1280]{1,0:T(8,128)(2,1)} %bitcast.34, bf16[320,1280]{1,0:T(8,128)(2,1)} %bitcast.47, bf16[320,1280]{1,0:T(8,128)(2,1)} %bitcast.66, ...), custom_call_target="tpu_custom_call" | custom-call | flops 419430400 | bytes 1 | tf_op jit(solution)/shard_map/weights_3/pallas_call | solution.py:423
  141.0 8.9 %collective-permute-done.17.refs_1_ = bf16[512,320]{1,0:T(8,128)(2,1)S(1)} collective-permute-done((bf16[512,320]{1,0:T(8,128)(2,1)S(1)}, bf16[512,320]{1,0:T(8,128)(2,1)S(1)}, u32[]{:S(2)}, u32[]{:S(2)}) %collective-permute-start.17) | collective-permute-done | bytes 327712 | tf_op jit(solution)/shard_map/ppermute | solution.py:485
  149.9 2.7 %returns_stage_2.1 = (bf16[320,320]{1,0:T(8,128)(2,1)}, bf16[320,320]{1,0:T(8,128)(2,1)}, bf16[256,320]{1,0:T(8,128)(2,1)}, bf16[256,320]{1,0:T(8,128)(2,1)}) custom-call(bf16[2,256,320]{2,1,0:T(8,128)(2,1)} %get-tuple-element.132.refs_0_, bf16[2,256,320]{2,1,0:T(8,128)(2,1)} %copy-done.5, ...), custom_call_target="tpu_custom_call", output_to_operand_aliasing={{0}: (4, {}), {1}: (5, {})} | custom-call | bytes 1 | tf_op jit(solution)/shard_map/returns_stage_2/pallas_call | solution.py:423
  152.7 1.7 collective-permute-done.19.b
  155.1 1.8 add_merges.3.a
  157.0 2.7 %collective-permute-start.20 = (bf16[320,320]{1,0:T(8,128)(2,1)}, bf16[320,320]{1,0:T(8,128)(2,1)S(1)}, u32[]{:S(2)}, u32[]{:S(2)}) collective-permute-start(bf16[320,320]{1,0:T(8,128)(2,1)} %add_merges.3.a), channel_id=1, source_target_pairs={{16,17},{17,16},{18,19},{19,18},{20,21},{21,20},{22,23},{23,22},{2... | collective-permute-start | bytes 614408 | tf_op jit(solution)/shard_map/ppermute | solution.py:485
  159.7 7.4 %collective-permute-done.20.b = bf16[320,320]{1,0:T(8,128)(2,1)S(1)} collective-permute-done((bf16[320,320]{1,0:T(8,128)(2,1)}, bf16[320,320]{1,0:T(8,128)(2,1)S(1)}, u32[]{:S(2)}, u32[]{:S(2)}) %collective-permute-start.20) | collective-permute-done | bytes 204832 | tf_op jit(solution)/shard_map/ppermute | solution.py:485
  167.8 1.9 add_merges.4.a
  169.7 2.5 %collective-permute-start.21 = (bf16[320,320]{1,0:T(8,128)(2,1)}, bf16[320,320]{1,0:T(8,128)(2,1)S(1)}, u32[]{:S(2)}, u32[]{:S(2)}) collective-permute-start(bf16[320,320]{1,0:T(8,128)(2,1)} %add_merges.4.a), channel_id=1, source_target_pairs={{16,18},{17,19},{18,16},{19,17},{20,22},{21,23},{22,20},{23,21},{2... | collective-permute-start | bytes 614408 | tf_op jit(solution)/shard_map/ppermute | solution.py:485
  172.5 8.0 %weights_2.1 = (f32[320,1280]{1,0:T(8,128)}, f32[320,1280]{1,0:T(8,128)}, f32[320,1280]{1,0:T(8,128)}) custom-call(bf16[4,528,320]{2,1,0:T(8,128)(2,1)} %bitcast.52, bf16[512,320]{1,0:T(8,128)(2,1)} %copy-done.16, bf16[320,1280]{1,0:T(8,128)(2,1)} %bitcast.35, bf16[320,1280]{1,0:T(8,128)(2,1)} %bitcast.48, bf16[320,1280]{1,0:T(8,128)(2,1)} %bitcast.67, ...), custom_call_target="tpu_custom_call" | custom-call | flops 419430400 | bytes 1 | tf_op jit(solution)/shard_map/weights_2/pallas_call | solution.py:423
  180.6 4.5 %collective-permute-done.21.b = bf16[320,320]{1,0:T(8,128)(2,1)S(1)} collective-permute-done((bf16[320,320]{1,0:T(8,128)(2,1)}, bf16[320,320]{1,0:T(8,128)(2,1)S(1)}, u32[]{:S(2)}, u32[]{:S(2)}) %collective-permute-start.21) | collective-permute-done | bytes 204832 | tf_op jit(solution)/shard_map/ppermute | solution.py:485
  185.8 1.9 add_merges.5
  187.7 1.8 select_bitcast_fusion
  (99 shorter events, 22.3 us)
Async XLA Ops:
  7.2 103.1 %all-gather.3.cloned.1.call-start = ((), (), s32[]{:S(2)}) async-start(), calls=%async_computation | async-start | bytes 2027520 | tf_op jit(solution)/shard_map/all_gather | solution.py:592
  7.2 4.3 %collective-permute-start = (bf16[320,1280]{1,0:T(8,128)(2,1)}, bf16[320,1280]{1,0:T(8,128)(2,1)S(1)}, u32[]{:S(2)}, u32[]{:S(2)}) collective-permute-start(bf16[320,1280]{1,0:T(8,128)(2,1)} %bitcast.23), channel_id=1, source_target_pairs={{0,4},{4,0},{8,12},{12,8},{16,20},{20,16},{24,28},{28,24},{1,5},{5... | collective-permute-start | bytes 2457608 | tf_op jit(solution)/shard_map/ppermute | solution.py:465
  7.3 4.2 %collective-permute-start.1 = (bf16[320,1280]{1,0:T(8,128)(2,1)}, bf16[320,1280]{1,0:T(8,128)(2,1)S(1)}, u32[]{:S(2)}, u32[]{:S(2)}) collective-permute-start(bf16[320,1280]{1,0:T(8,128)(2,1)} %bitcast.36), channel_id=1, source_target_pairs={{0,4},{4,0},{8,12},{12,8},{16,20},{20,16},{24,28},{28,24},{1,5},{5... | collective-permute-start | bytes 2457608 | tf_op jit(solution)/shard_map/ppermute | solution.py:465
  7.8 3.7 %collective-permute-start.3 = (bf16[320,320]{1,0:T(8,128)(2,1)}, bf16[320,320]{1,0:T(8,128)(2,1)S(1)}, u32[]{:S(2)}, u32[]{:S(2)}) collective-permute-start(bf16[320,320]{1,0:T(8,128)(2,1)} %bitcast.53), channel_id=1, source_target_pairs={{0,4},{4,0},{8,12},{12,8},{16,20},{20,16},{24,28},{28,24},{1,5},{5... | collective-permute-start | bytes 614408 | tf_op jit(solution)/shard_map/ppermute | solution.py:465
  10.1 1.4 collective-permute-start.2
  13.0 7.4 %collective-permute-start.4 = (bf16[256,320]{1,0:T(8,128)(2,1)}, bf16[256,320]{1,0:T(8,128)(2,1)S(1)}, u32[]{:S(2)}, u32[]{:S(2)}) collective-permute-start(bf16[256,320]{1,0:T(8,128)(2,1)} %get-tuple-element.71), channel_id=1, source_target_pairs={{0,8},{4,12},{8,0},{12,4},{16,24},{20,28},{24,16},{28,20},{1,9},{5... | collective-permute-start | bytes 491528 | tf_op jit(solution)/shard_map/ppermute | solution.py:471
  21.1 10.8 %copy-start.25 = (bf16[2,256,320]{2,1,0:T(8,128)(2,1)S(1)}, bf16[2,256,320]{2,1,0:T(8,128)(2,1)}, u32[]{:S(2)}) copy-start(bf16[2,256,320]{2,1,0:T(8,128)(2,1)} %get-tuple-element.84) | copy-start | bytes 983044
  21.3 19.7 %collective-permute-start.5 = (bf16[2,256,320]{2,1,0:T(8,128)(2,1)}, bf16[2,256,320]{2,1,0:T(8,128)(2,1)S(1)}, u32[]{:S(2)}, u32[]{:S(2)}) collective-permute-start(bf16[2,256,320]{2,1,0:T(8,128)(2,1)} %get-tuple-element.77), channel_id=1, source_target_pairs={{8,16},{12,20},{16,8},{20,12},{9,17},{13,21},{17,9},{21,13},{10,18... | collective-permute-start | bytes 983048 | tf_op jit(solution)/shard_map/ppermute | solution.py:477
  31.9 15.4 %collective-permute-start.7 = (bf16[2,256,320]{2,1,0:T(8,128)(2,1)S(1)}, bf16[2,256,320]{2,1,0:T(8,128)(2,1)S(1)}, u32[]{:S(2)}, u32[]{:S(2)}) collective-permute-start(bf16[2,256,320]{2,1,0:T(8,128)(2,1)S(1)} %copy-done.25), channel_id=1, source_target_pairs={{0,24},{4,28},{24,0},{28,4},{1,25},{5,29},{25,1},{29,5},{2,26},{6,... | collective-permute-start | bytes 983048 | tf_op jit(solution)/shard_map/ppermute | solution.py:477
  47.2 6.1 %collective-permute-start.6 = (bf16[256,320]{1,0:T(8,128)(2,1)}, bf16[256,320]{1,0:T(8,128)(2,1)S(1)}, u32[]{:S(2)}, u32[]{:S(2)}) collective-permute-start(bf16[256,320]{1,0:T(8,128)(2,1)} %get-tuple-element.83), channel_id=1, source_target_pairs={{0,8},{4,12},{8,0},{12,4},{16,24},{20,28},{24,16},{28,20},{1,9},{5... | collective-permute-start | bytes 491528 | tf_op jit(solution)/shard_map/ppermute | solution.py:471
  47.3 6.1 %copy-start.9 = (bf16[2,256,320]{2,1,0:T(8,128)(2,1)}, bf16[2,256,320]{2,1,0:T(8,128)(2,1)S(1)}, u32[]{:S(2)}) copy-start(bf16[2,256,320]{2,1,0:T(8,128)(2,1)S(1)} %collective-permute-done.7.refs_1_) | copy-start | bytes 983044
  54.7 16.2 %copy-start.8 = (bf16[256,320]{1,0:T(8,128)(2,1)S(1)}, bf16[256,320]{1,0:T(8,128)(2,1)}, u32[]{:S(2)}) copy-start(bf16[256,320]{1,0:T(8,128)(2,1)} %get-tuple-element.100) | copy-start | bytes 491524
  55.2 1.4 collective-permute-start.9
  57.6 18.6 %collective-permute-start.8 = (bf16[256,320]{1,0:T(8,128)(2,1)S(1)}, bf16[256,320]{1,0:T(8,128)(2,1)S(1)}, u32[]{:S(2)}, u32[]{:S(2)}) collective-permute-start(bf16[256,320]{1,0:T(8,128)(2,1)S(1)} %copy-done.26), channel_id=1, source_target_pairs={{0,8},{4,12},{8,0},{12,4},{16,24},{20,28},{24,16},{28,20},{1,9},{5... | collective-permute-start | bytes 491528 | tf_op jit(solution)/shard_map/ppermute | solution.py:471
  70.9 5.2 %collective-permute-start.10 = (bf16[256,320]{1,0:T(8,128)(2,1)S(1)}, bf16[256,320]{1,0:T(8,128)(2,1)S(1)}, u32[]{:S(2)}, u32[]{:S(2)}) collective-permute-start(bf16[256,320]{1,0:T(8,128)(2,1)S(1)} %copy-done.8), channel_id=1, source_target_pairs={{0,4},{4,0},{8,12},{12,8},{16,20},{20,16},{24,28},{28,24},{1,5},{5... | collective-permute-start | bytes 491528 | tf_op jit(solution)/shard_map/ppermute | solution.py:465
  70.9 11.2 %collective-permute-start.11 = (bf16[256,320]{1,0:T(8,128)(2,1)}, bf16[256,320]{1,0:T(8,128)(2,1)S(1)}, u32[]{:S(2)}, u32[]{:S(2)}) collective-permute-start(bf16[256,320]{1,0:T(8,128)(2,1)} %get-tuple-element.105), channel_id=1, source_target_pairs={{24,8},{28,12},{8,24},{12,28},{25,9},{29,13},{9,25},{13,29},{26,10... | collective-permute-start | bytes 491528 | tf_op jit(solution)/shard_map/ppermute | solution.py:477
  71.6 10.6 %collective-permute-start.12 = (bf16[256,320]{1,0:T(8,128)(2,1)}, bf16[256,320]{1,0:T(8,128)(2,1)S(1)}, u32[]{:S(2)}, u32[]{:S(2)}) collective-permute-start(bf16[256,320]{1,0:T(8,128)(2,1)} %get-tuple-element.98), channel_id=1, source_target_pairs={{24,0},{28,4},{0,24},{4,28},{25,1},{29,5},{1,25},{5,29},{26,2},{30... | collective-permute-start | bytes 491528 | tf_op jit(solution)/shard_map/ppermute | solution.py:477
  76.1 6.0 %copy-start.15 = (bf16[256,320]{1,0:T(8,128)(2,1)}, bf16[256,320]{1,0:T(8,128)(2,1)S(1)}, u32[]{:S(2)}) copy-start(bf16[256,320]{1,0:T(8,128)(2,1)S(1)} %collective-permute-done.10.refs_1_) | copy-start | bytes 491524
  82.1 13.7 %copy-start.24 = (bf16[256,320]{1,0:T(8,128)(2,1)}, bf16[256,320]{1,0:T(8,128)(2,1)S(1)}, u32[]{:S(2)}) copy-start(bf16[256,320]{1,0:T(8,128)(2,1)S(1)} %collective-permute-done.11.refs_5_) | copy-start | bytes 491524
  82.2 14.6 %copy-start.22 = (bf16[256,320]{1,0:T(8,128)(2,1)}, bf16[256,320]{1,0:T(8,128)(2,1)S(1)}, u32[]{:S(2)}) copy-start(bf16[256,320]{1,0:T(8,128)(2,1)S(1)} %collective-permute-done.12.refs_4_) | copy-start | bytes 491524
  82.2 13.7 %collective-permute-start.13 = (bf16[2,256,320]{2,1,0:T(8,128)(2,1)}, bf16[2,256,320]{2,1,0:T(8,128)(2,1)S(1)}, u32[]{:S(2)}, u32[]{:S(2)}) collective-permute-start(bf16[2,256,320]{2,1,0:T(8,128)(2,1)} %get-tuple-element.106), channel_id=1, source_target_pairs={{16,8},{20,12},{8,16},{12,20},{17,9},{21,13},{9,17},{13,21},{18,10... | collective-permute-start | bytes 983048 | tf_op jit(solution)/shard_map/ppermute | solution.py:477
  96.8 5.9 %collective-permute-start.14 = (bf16[256,320]{1,0:T(8,128)(2,1)}, bf16[256,320]{1,0:T(8,128)(2,1)S(1)}, u32[]{:S(2)}, u32[]{:S(2)}) collective-permute-start(bf16[256,320]{1,0:T(8,128)(2,1)} %get-tuple-element.110), channel_id=1, source_target_pairs={{0,8},{4,12},{8,0},{12,4},{16,24},{20,28},{24,16},{28,20},{1,9},{5... | collective-permute-start | bytes 491528 | tf_op jit(solution)/shard_map/ppermute | solution.py:471
  102.8 7.5 %copy-start.13 = (bf16[256,320]{1,0:T(8,128)(2,1)}, bf16[256,320]{1,0:T(8,128)(2,1)S(1)}, u32[]{:S(2)}) copy-start(bf16[256,320]{1,0:T(8,128)(2,1)S(1)} %collective-permute-done.14.refs_0_.refs_5_) | copy-start | bytes 491524
  110.5 1.7 collective-permute-start.15
  112.2 4.2 %copy-start.12 = (bf16[512,320]{1,0:T(8,128)(2,1)}, bf16[512,320]{1,0:T(8,128)(2,1)S(1)}, u32[]{:S(2)}) copy-start(bf16[512,320]{1,0:T(8,128)(2,1)S(1)} %constant_dynamic-update-slice_fusion.refs_1_) | copy-start | bytes 983044
  112.2 11.3 %collective-permute-start.16 = (bf16[512,320]{1,0:T(8,128)(2,1)S(1)}, bf16[512,320]{1,0:T(8,128)(2,1)S(1)}, u32[]{:S(2)}, u32[]{:S(2)}) collective-permute-start(bf16[512,320]{1,0:T(8,128)(2,1)S(1)} %constant_dynamic-update-slice_fusion.refs_1_), channel_id=1, source_target_pairs={{0,1},{1,0},{2,3},{3,2},{4,5},{5,4},{6,7},{7,6},{8,9},{9,8},{10,11... | collective-permute-start | bytes 983048 | tf_op jit(solution)/shard_map/ppermute | solution.py:485
  112.7 20.8 %collective-permute-start.18 = (bf16[512,320]{1,0:T(8,128)(2,1)S(1)}, bf16[512,320]{1,0:T(8,128)(2,1)S(1)}, u32[]{:S(2)}, u32[]{:S(2)}) collective-permute-start(bf16[512,320]{1,0:T(8,128)(2,1)S(1)} %constant_dynamic-update-slice_fusion.refs_1_), channel_id=1, source_target_pairs={{0,3},{1,2},{2,1},{3,0},{4,7},{5,6},{6,5},{7,4},{8,11},{9,10},{10,... | collective-permute-start | bytes 983048 | tf_op jit(solution)/shard_map/ppermute | solution.py:485
  115.0 34.9 %collective-permute-start.17 = (bf16[512,320]{1,0:T(8,128)(2,1)S(1)}, bf16[512,320]{1,0:T(8,128)(2,1)S(1)}, u32[]{:S(2)}, u32[]{:S(2)}) collective-permute-start(bf16[512,320]{1,0:T(8,128)(2,1)S(1)} %constant_dynamic-update-slice_fusion.refs_1_), channel_id=1, source_target_pairs={{0,2},{1,3},{2,0},{3,1},{4,6},{5,7},{6,4},{7,5},{8,10},{9,11},{10,... | collective-permute-start | bytes 983048 | tf_op jit(solution)/shard_map/ppermute | solution.py:485
  149.9 22.2 %copy-start.16 = (bf16[512,320]{1,0:T(8,128)(2,1)}, bf16[512,320]{1,0:T(8,128)(2,1)S(1)}, u32[]{:S(2)}) copy-start(bf16[512,320]{1,0:T(8,128)(2,1)S(1)} %collective-permute-done.17.refs_1_) | copy-start | bytes 983044
  152.6 1.8 collective-permute-start.19
  157.0 10.1 %collective-permute-start.20 = (bf16[320,320]{1,0:T(8,128)(2,1)}, bf16[320,320]{1,0:T(8,128)(2,1)S(1)}, u32[]{:S(2)}, u32[]{:S(2)}) collective-permute-start(bf16[320,320]{1,0:T(8,128)(2,1)} %add_merges.3.a), channel_id=1, source_target_pairs={{16,17},{17,16},{18,19},{19,18},{20,21},{21,20},{22,23},{23,22},{2... | collective-permute-start | bytes 614408 | tf_op jit(solution)/shard_map/ppermute | solution.py:485
  169.7 15.4 %collective-permute-start.21 = (bf16[320,320]{1,0:T(8,128)(2,1)}, bf16[320,320]{1,0:T(8,128)(2,1)S(1)}, u32[]{:S(2)}, u32[]{:S(2)}) collective-permute-start(bf16[320,320]{1,0:T(8,128)(2,1)} %add_merges.4.a), channel_id=1, source_target_pairs={{16,18},{17,19},{18,16},{19,17},{20,22},{21,23},{22,20},{23,21},{2... | collective-permute-start | bytes 614408 | tf_op jit(solution)/shard_map/ppermute | solution.py:485
  (18 other events, 18.3 us)
Sparse Core Ops, SparseCore 0:
  57.7 52.5 all-gather.2

commit v3 on v2

--- a/solution.py
+++ b/solution.py
@@ -381,16 +381,29 @@
         copy.wait()
 
 
-def add_kernel(half, a, b, out, here, semaphores):
+def add_kernel(half, *refs):
+    count = len(refs) - 4
+    out, here, result, semaphores = refs[count:]
     stage, core = place()
 
     @pl.when(stage >= half)
     def _():
         copies = Copies(semaphores, core)
-        for copy in [copies.start(a, here.at[0]), copies.start(b, here.at[1])]:
+        for copy in [copies.start(ref, here.at[i]) for i, ref in enumerate(refs[:count])]:
             copy.wait()
-        here[2] = added(here[0], here[1])
-        copies.start(here.at[2], out).wait()
+        values = [here[i].astype(F32) for i in range(count)]
+        while len(values) > 1:
+            values = [a + b for a, b in zip(values[::2], values[1::2])]
+        result[...] = values[0].astype(result.dtype)
+        copies.start(result, out).wait()
+
+    if out.dtype == F32:
+
+        @pl.when(stage < half)
+        def _():
+            result[...] = jnp.zeros(result.shape, F32)
+            copy = Copies(semaphores, core).start(result, out)
+            copy.wait()
 
 
 def assemble_kernel(turns, n_alias, *refs):
@@ -604,20 +617,16 @@
 
     outputs = assemble([(0, 0), (half, stages - 1)], None, sent)
 
-    def add(a, b):
+    def add(*values, dtype=BF16):
+        scratch = [pltpu.VMEM((len(values), width, width), BF16), pltpu.VMEM((width, width), dtype)]
         return call(
-            functools.partial(add_kernel, half), [a, b], [shape((width, width))],
-            [pltpu.VMEM((3, width, width), BF16), pltpu.SemaphoreType.DMA((4,))], None, 0, "add_merges",
+            functools.partial(add_kernel, half), list(values), [shape((width, width), dtype)],
+            scratch + [pltpu.SemaphoreType.DMA((len(values) + 1,))], None, 0, "add_merges",
         )[0]
 
-    def merge_gradients(waited):
-        keep, send = returns(half, after(middle_grads, *waited), waited[0])[:2]
-        total = add(keep, swap_cores(send))
-        distance = 1
-        while distance < replicas:
-            total = add(total, over_replicas(total, distance, high_stages))
-            distance *= 2
-        return total
+    def merge_gradients(total):
+        came = {d: over_replicas(total, d, high_stages) for d in distances}
+        return add(total, *[came[d] for d in range(1, replicas)], dtype=F32)
 
     for stage in range(half - 1, -1, -1):
         extra_b = back_pairs[stage - 1][0] if stage > 0 else arrived
@@ -630,8 +639,6 @@
         )
         if stage > 0:
             arrived = hop_between(sent, stage - 1)
-        if stage == 1:
-            arrived = after(arrived, gathered)
 
     kept_grad, sent_grad = kept
     came_grad = swap_cores(sent_grad)
@@ -669,10 +676,12 @@
         if not last:
             stack.append(result[0])
             sums = tuple(result[1:])
+        if count == 1:
+            keep, send = returns(half, middle_grads, sums[0])[:2]
+            total = add(keep, swap_cores(send))
     grad_first, grad_second, grad_clock = result
 
-    total = merge_gradients((grads[distances[-1]], sums[0]))
-    grad_merge = jnp.where(rank // 2 < half, 0.0, total.astype(F32))
+    grad_merge = merge_gradients(after(total, grads[distances[-1]], sums[0]))
     return (
         outputs.transpose(0, 2, 1)[None],
         grad_first[None],

time: 197 us -> 183 us (0.929)
  waiting for transfers between devices: 74.2 us -> 55.2 us
  starting transfers between devices: 41.1 us -> 49.3 us
    ppermute x5 -> x6, waiting for transfers between devices: 23.7 us -> 13.9 us  [over_replicas(): return lax.ppermute(block, ('section', 'dp'), route)]
    ppermute x5 -> x6, starting transfers between devices: 8.72 us -> 16.9 us  [over_replicas(): return lax.ppermute(block, ('section', 'dp'), route)]
    all_gather x1, waiting for transfers between devices: 7.48 us -> 0.01 us  [local(): gathered = lax.all_gather(packed, 'dp')]
    pallas_call x19 -> x18, Pallas kernels: 51.2 us -> 49.6 us  [call(): pl.pallas_call(kernel, out_shape=outs, in_specs=[IN_HBM] * len(args), out...]
    unnamed x55 -> x57, local copies, waits for them, and re-layouts: 9.67 us -> 10.3 us
  transfers between devices with their start and end apart: 23 -> 24, of which waited for: 16 -> 12; matrix products, arithmetic and copies ran while one was open for 2% -> 2% of each run, Pallas kernels for 21% -> 25%
where the time goes in v3:
time: 183 us
  waiting for transfers between devices  55.2 us (30%)
  Pallas kernels  49.6 us (27%)
  starting transfers between devices  49.3 us (27%)
  between operations  14.5 us (8%)
  local copies, waits for them, and re-layouts  10.4 us (6%)
  other arithmetic  2.36 us (1%)
    pallas_call x18, Pallas kernels, call(): pl.pallas_call(kernel, out_shape=outs, in_specs=[IN_HBM] * len(args), out...  49.6 us
    ppermute x4, waiting for transfers between devices, hop_between(): lax.ppermute(block, 'section', [(2 * a + c, 2 * b + c) for a, b in pairs....  21.6 us
    ppermute x6, starting transfers between devices, over_replicas(): return lax.ppermute(block, ('section', 'dp'), route)  16.9 us
    ppermute x5, waiting for transfers between devices, between(): lax.ppermute(block, 'section', [(2 * i + c, 2 * j + c) for i, j in pairs...  16.6 us
    ppermute x5, starting transfers between devices, between(): lax.ppermute(block, 'section', [(2 * i + c, 2 * j + c) for i, j in pairs...  16 us
    ppermute x4, starting transfers between devices, hop_between(): lax.ppermute(block, 'section', [(2 * a + c, 2 * b + c) for a, b in pairs....  15 us
    ppermute x6, waiting for transfers between devices, over_replicas(): return lax.ppermute(block, ('section', 'dp'), route)  13.9 us
    unnamed x57, local copies, waits for them, and re-layouts  10.3 us
  transfers between devices with their start and end apart: 24, of which 12 were waited for; matrix products, arithmetic and copies ran while one was open for 2% of the time, Pallas kernels for 25%

profile of v3, /device:TPU:4, one launch (start us, length us, event | category | flops | bytes accessed | tf_op | source)
XLA Modules:
  0.0 182.8 jit_solution(2742725577168986578)
XLA Ops:
  8.7 1.4 fusion.5.refs_4_
  10.6 0.9 collective-permute-done.2.refs_8_
  13.0 1.6 collective-permute-start.4
  14.5 5.9 %collective-permute-done.4.refs_0_.refs_1_ = bf16[256,320]{1,0:T(8,128)(2,1)S(1)} collective-permute-done((bf16[256,320]{1,0:T(8,128)(2,1)}, bf16[256,320]{1,0:T(8,128)(2,1)S(1)}, u32[]{:S(2)}, u32[]{:S(2)}) %collective-permute-start.4) | collective-permute-done | bytes 163872 | tf_op jit(solution)/shard_map/ppermute | solution.py:484
  21.3 10.6 %collective-permute-start.5 = (bf16[2,256,320]{2,1,0:T(8,128)(2,1)}, bf16[2,256,320]{2,1,0:T(8,128)(2,1)S(1)}, u32[]{:S(2)}, u32[]{:S(2)}) collective-permute-start(bf16[2,256,320]{2,1,0:T(8,128)(2,1)} %get-tuple-element.76), channel_id=1, source_target_pairs={{8,16},{12,20},{16,8},{20,12},{9,17},{13,21},{17,9},{21,13},{10,18... | collective-permute-start | bytes 983048 | tf_op jit(solution)/shard_map/ppermute | solution.py:490
  32.6 8.4 %collective-permute-done.5.refs_0_.refs_1_ = bf16[2,256,320]{2,1,0:T(8,128)(2,1)S(1)} collective-permute-done((bf16[2,256,320]{2,1,0:T(8,128)(2,1)}, bf16[2,256,320]{2,1,0:T(8,128)(2,1)S(1)}, u32[]{:S(2)}, u32[]{:S(2)}) %collective-permute-start.5) | collective-permute-done | bytes 327712 | tf_op jit(solution)/shard_map/ppermute | solution.py:490
  41.8 5.4 %forward_stage_2.1 = (bf16[256,320]{1,0:T(8,128)(2,1)}, bf16[256,320]{1,0:T(8,128)(2,1)}, bf16[256,320]{1,0:T(8,128)(2,1)}, bf16[2,256,320]{2,1,0:T(8,128)(2,1)}...) custom-call(bf16[2,256,320]{2,1,0:T(8,128)(2,1)} %copy-done.5, ...), custom_call_target="tpu_custom_call", output_to_operand_aliasing={{1}: (10, {}), {2}: (11, {}), {4}: (12, {}), {5}: (13, {}),... | custom-call | bytes 1 | tf_op jit(solution)/shard_map/forward_stage_2/pallas_call | solution.py:436
  47.3 6.0 %collective-permute-done.6.refs_0_ = bf16[256,320]{1,0:T(8,128)(2,1)S(1)} collective-permute-done((bf16[256,320]{1,0:T(8,128)(2,1)}, bf16[256,320]{1,0:T(8,128)(2,1)S(1)}, u32[]{:S(2)}, u32[]{:S(2)}) %collective-permute-start.6) | collective-permute-done | bytes 163872 | tf_op jit(solution)/shard_map/ppermute | solution.py:484
  55.3 1.4 collective-permute-done.9
  56.6 0.9 maximum_maximum_fusion
  57.6 13.3 %collective-permute-start.8 = (bf16[256,320]{1,0:T(8,128)(2,1)S(1)}, bf16[256,320]{1,0:T(8,128)(2,1)S(1)}, u32[]{:S(2)}, u32[]{:S(2)}) collective-permute-start(bf16[256,320]{1,0:T(8,128)(2,1)S(1)} %copy-done.27), channel_id=1, source_target_pairs={{0,8},{4,12},{8,0},{12,4},{16,24},{20,28},{24,16},{28,20},{1,9},{5... | collective-permute-start | bytes 491528 | tf_op jit(solution)/shard_map/ppermute | solution.py:484
  72.2 3.8 %collective-permute-done.8.refs_0_.refs_4_.refs_5_ = bf16[256,320]{1,0:T(8,128)(2,1)S(1)} collective-permute-done((bf16[256,320]{1,0:T(8,128)(2,1)S(1)}, bf16[256,320]{1,0:T(8,128)(2,1)S(1)}, u32[]{:S(2)}, u32[]{:S(2)}) %collective-permute-start.8) | collective-permute-done | bytes 163872 | tf_op jit(solution)/shard_map/ppermute | solution.py:484
  76.8 5.3 %backward_stage_2.1 = (bf16[256,320]{1,0:T(8,128)(2,1)}, bf16[256,320]{1,0:T(8,128)(2,1)}, bf16[256,320]{1,0:T(8,128)(2,1)}, bf16[2,256,320]{2,1,0:T(8,128)(2,1)}, bf16[2,256,320]{2,1,0:T(8,128)(2,1)}) custom-call(bf16[256,320]{1,0:T(8,128)(2,1)} %copy-done.7, ...), custom_call_target="tpu_custom_call", output_to_operand_aliasing={{1}: (12, {}), {2}: (13, {})} | custom-call | bytes 1 | tf_op jit(solution)/shard_map/backward_stage_2/pallas_call | solution.py:436
  82.1 3.5 %collective-permute-start.13 = (bf16[2,256,320]{2,1,0:T(8,128)(2,1)}, bf16[2,256,320]{2,1,0:T(8,128)(2,1)S(1)}, u32[]{:S(2)}, u32[]{:S(2)}) collective-permute-start(bf16[2,256,320]{2,1,0:T(8,128)(2,1)} %get-tuple-element.105), channel_id=1, source_target_pairs={{16,8},{20,12},{8,16},{12,20},{17,9},{21,13},{9,17},{13,21},{18,10... | collective-permute-start | bytes 983048 | tf_op jit(solution)/shard_map/ppermute | solution.py:490
  85.6 2.0 %outputs_0_2.1.refs_2_ = bf16[4,320,128]{2,1,0:T(8,128)(2,1)} custom-call(bf16[256,320]{1,0:T(8,128)(2,1)} %get-tuple-element.115.refs_0_, bf16[256,320]{1,0:T(8,128)(2,1)} %copy-done.15), custom_call_target="tpu_custom_call" | custom-call | bytes 1 | tf_op jit(solution)/shard_map/outputs_0_2/pallas_call | solution.py:436
  87.6 8.2 %collective-permute-done.13.refs_0_.refs_4_ = bf16[2,256,320]{2,1,0:T(8,128)(2,1)S(1)} collective-permute-done((bf16[2,256,320]{2,1,0:T(8,128)(2,1)}, bf16[2,256,320]{2,1,0:T(8,128)(2,1)S(1)}, u32[]{:S(2)}, u32[]{:S(2)}) %collective-permute-start.13) | collective-permute-done | bytes 327712 | tf_op jit(solution)/shard_map/ppermute | solution.py:490
  96.9 5.9 %collective-permute-done.14.refs_0_.refs_5_ = bf16[256,320]{1,0:T(8,128)(2,1)S(1)} collective-permute-done((bf16[256,320]{1,0:T(8,128)(2,1)}, bf16[256,320]{1,0:T(8,128)(2,1)S(1)}, u32[]{:S(2)}, u32[]{:S(2)}) %collective-permute-start.14) | collective-permute-done | bytes 163872 | tf_op jit(solution)/shard_map/ppermute | solution.py:484
  103.7 0.9 constant_dynamic-update-slice_fusion.1
  105.4 3.5 %collective-permute-start.16 = (bf16[512,320]{1,0:T(8,128)(2,1)S(1)}, bf16[512,320]{1,0:T(8,128)(2,1)S(1)}, u32[]{:S(2)}, u32[]{:S(2)}) collective-permute-start(bf16[512,320]{1,0:T(8,128)(2,1)S(1)} %constant_dynamic-update-slice_fusion.refs_1_), channel_id=1, source_target_pairs={{0,1},{1,0},{2,3},{3,2},{4,5},{5,4},{6,7},{7,6},{8,9},{9,8},{10,11... | collective-permute-start | bytes 983048 | tf_op jit(solution)/shard_map/ppermute | solution.py:498
  108.9 2.5 %collective-permute-start.18 = (bf16[512,320]{1,0:T(8,128)(2,1)S(1)}, bf16[512,320]{1,0:T(8,128)(2,1)S(1)}, u32[]{:S(2)}, u32[]{:S(2)}) collective-permute-start(bf16[512,320]{1,0:T(8,128)(2,1)S(1)} %constant_dynamic-update-slice_fusion.refs_1_), channel_id=1, source_target_pairs={{0,3},{1,2},{2,1},{3,0},{4,7},{5,6},{6,5},{7,4},{8,11},{9,10},{10,... | collective-permute-start | bytes 983048 | tf_op jit(solution)/shard_map/ppermute | solution.py:498
  112.2 6.6 %weights_0.1 = (f32[2,320,1280]{2,1,0:T(8,128)}, f32[4,16,1280]{2,1,0:T(8,128)}, bf16[4,16,320]{2,1,0:T(8,128)(2,1)}) custom-call(bf16[4,528,320]{2,1,0:T(8,128)(2,1)} %bitcast.48, bf16[512,320]{1,0:T(8,128)(2,1)} %copy-done.12, bf16[320,1280]{1,0:T(8,128)(2,1)} %bitcast.31, bf16[320,1280]{1,0:T(8,128)(2,1)} %bitcast.44, bf16[320,1280]{1,0:T(8,128)(2,1)} %bitcast.63, ...), custom_call_target="tpu_custom_call" | custom-call | flops 419430400 | bytes 1 | tf_op jit(solution)/shard_map/weights_0/pallas_call | solution.py:436
  119.5 7.0 %weights_1.1 = (f32[2,320,1280]{2,1,0:T(8,128)}, f32[4,16,1280]{2,1,0:T(8,128)}, bf16[4,16,320]{2,1,0:T(8,128)(2,1)}) custom-call(bf16[4,528,320]{2,1,0:T(8,128)(2,1)} %bitcast.49, bf16[512,320]{1,0:T(8,128)(2,1)} %copy-done.17, bf16[320,1280]{1,0:T(8,128)(2,1)} %bitcast.32, bf16[320,1280]{1,0:T(8,128)(2,1)} %bitcast.45, bf16[320,1280]{1,0:T(8,128)(2,1)} %bitcast.64, ...), custom_call_target="tpu_custom_call" | custom-call | flops 419430400 | bytes 1 | tf_op jit(solution)/shard_map/weights_1/pallas_call | solution.py:436
  126.5 2.6 %returns_stage_2.1 = (bf16[320,320]{1,0:T(8,128)(2,1)}, bf16[320,320]{1,0:T(8,128)(2,1)}, bf16[256,320]{1,0:T(8,128)(2,1)}, bf16[256,320]{1,0:T(8,128)(2,1)}) custom-call(bf16[2,256,320]{2,1,0:T(8,128)(2,1)} %get-tuple-element.129.refs_0_, bf16[2,256,320]{2,1,0:T(8,128)(2,1)} %copy-done.5, ...), custom_call_target="tpu_custom_call", output_to_operand_aliasing={{0}: (4, {}), {1}: (5, {})} | custom-call | bytes 1 | tf_op jit(solution)/shard_map/returns_stage_2/pallas_call | solution.py:436
  130.6 6.7 %weights_3.1 = (f32[2,320,1280]{2,1,0:T(8,128)}, f32[4,16,1280]{2,1,0:T(8,128)}, bf16[4,16,320]{2,1,0:T(8,128)(2,1)}) custom-call(bf16[4,528,320]{2,1,0:T(8,128)(2,1)} %bitcast.50, bf16[512,320]{1,0:T(8,128)(2,1)} %copy-done.18, bf16[320,1280]{1,0:T(8,128)(2,1)} %bitcast.33, bf16[320,1280]{1,0:T(8,128)(2,1)} %bitcast.46, bf16[320,1280]{1,0:T(8,128)(2,1)} %bitcast.65, ...), custom_call_target="tpu_custom_call" | custom-call | flops 419430400 | bytes 1 | tf_op jit(solution)/shard_map/weights_3/pallas_call | solution.py:436
  138.0 1.8 %add_merges.2.refs_0_ = bf16[320,320]{1,0:T(8,128)(2,1)} custom-call(bf16[320,320]{1,0:T(8,128)(2,1)} %get-tuple-element.132.refs_0_, bf16[320,320]{1,0:T(8,128)(2,1)} %copy-done.22), custom_call_target="tpu_custom_call" | custom-call | bytes 1 | tf_op jit(solution)/shard_map/add_merges/pallas_call | solution.py:436
  139.9 6.1 %collective-permute-done.17.refs_1_ = bf16[512,320]{1,0:T(8,128)(2,1)S(1)} collective-permute-done((bf16[512,320]{1,0:T(8,128)(2,1)S(1)}, bf16[512,320]{1,0:T(8,128)(2,1)S(1)}, u32[]{:S(2)}, u32[]{:S(2)}) %collective-permute-start.17) | collective-permute-done | bytes 327712 | tf_op jit(solution)/shard_map/ppermute | solution.py:498
  145.9 6.2 %collective-permute-start.22 = (bf16[320,320]{1,0:T(8,128)(2,1)}, bf16[320,320]{1,0:T(8,128)(2,1)S(1)}, u32[]{:S(2)}, u32[]{:S(2)}) collective-permute-start(bf16[320,320]{1,0:T(8,128)(2,1)} %add_merges.2.refs_0_), channel_id=1, source_target_pairs={{16,19},{17,18},{18,17},{19,16},{20,23},{21,22},{22,21},{23,20},{2... | collective-permute-start | bytes 614408 | tf_op jit(solution)/shard_map/ppermute | solution.py:498
  152.1 2.1 %collective-permute-start.21 = (bf16[320,320]{1,0:T(8,128)(2,1)}, bf16[320,320]{1,0:T(8,128)(2,1)S(1)}, u32[]{:S(2)}, u32[]{:S(2)}) collective-permute-start(bf16[320,320]{1,0:T(8,128)(2,1)} %add_merges.2.refs_0_), channel_id=1, source_target_pairs={{16,18},{17,19},{18,16},{19,17},{20,22},{21,23},{22,20},{23,21},{2... | collective-permute-start | bytes 614408 | tf_op jit(solution)/shard_map/ppermute | solution.py:498
  154.3 2.5 %collective-permute-start.20 = (bf16[320,320]{1,0:T(8,128)(2,1)}, bf16[320,320]{1,0:T(8,128)(2,1)S(1)}, u32[]{:S(2)}, u32[]{:S(2)}) collective-permute-start(bf16[320,320]{1,0:T(8,128)(2,1)} %add_merges.2.refs_0_), channel_id=1, source_target_pairs={{16,17},{17,16},{18,19},{19,18},{20,21},{21,20},{22,23},{23,22},{2... | collective-permute-start | bytes 614408 | tf_op jit(solution)/shard_map/ppermute | solution.py:498
  157.1 8.0 %weights_2.1 = (f32[320,1280]{1,0:T(8,128)}, f32[320,1280]{1,0:T(8,128)}, f32[320,1280]{1,0:T(8,128)}) custom-call(bf16[4,528,320]{2,1,0:T(8,128)(2,1)} %bitcast.51, bf16[512,320]{1,0:T(8,128)(2,1)} %copy-done.16, bf16[320,1280]{1,0:T(8,128)(2,1)} %bitcast.34, bf16[320,1280]{1,0:T(8,128)(2,1)} %bitcast.47, bf16[320,1280]{1,0:T(8,128)(2,1)} %bitcast.66, ...), custom_call_target="tpu_custom_call" | custom-call | flops 419430400 | bytes 1 | tf_op jit(solution)/shard_map/weights_2/pallas_call | solution.py:436
  165.1 7.2 %collective-permute-done.21.refs_2_ = bf16[320,320]{1,0:T(8,128)(2,1)S(1)} collective-permute-done((bf16[320,320]{1,0:T(8,128)(2,1)}, bf16[320,320]{1,0:T(8,128)(2,1)S(1)}, u32[]{:S(2)}, u32[]{:S(2)}) %collective-permute-start.21) | collective-permute-done | bytes 204832 | tf_op jit(solution)/shard_map/ppermute | solution.py:498
  173.7 2.2 %add_merges.3 = f32[320,320]{1,0:T(8,128)} custom-call(bf16[320,320]{1,0:T(8,128)(2,1)} %add_merges.2.refs_0_, bf16[320,320]{1,0:T(8,128)(2,1)} %copy-done.21, bf16[320,320]{1,0:T(8,128)(2,1)} %copy-done.20, bf16[320,320]{1,0:T(8,128)(2,1)} %copy-done.19), custom_call_target="tpu_custom_call" | custom-call | bytes 1 | tf_op jit(solution)/shard_map/add_merges/pallas_call | solution.py:436
  (101 shorter events, 17.9 us)
Async XLA Ops:
  7.2 105.0 %all-gather.3.cloned.1.call-start = ((), (), s32[]{:S(2)}) async-start(), calls=%async_computation | async-start | bytes 2027520 | tf_op jit(solution)/shard_map/all_gather | solution.py:605
  7.2 4.3 %collective-permute-start.3 = (bf16[320,320]{1,0:T(8,128)(2,1)}, bf16[320,320]{1,0:T(8,128)(2,1)S(1)}, u32[]{:S(2)}, u32[]{:S(2)}) collective-permute-start(bf16[320,320]{1,0:T(8,128)(2,1)} %bitcast.52), channel_id=1, source_target_pairs={{0,4},{4,0},{8,12},{12,8},{16,20},{20,16},{24,28},{28,24},{1,5},{5... | collective-permute-start | bytes 614408 | tf_op jit(solution)/shard_map/ppermute | solution.py:478
  7.3 4.2 %collective-permute-start = (bf16[320,1280]{1,0:T(8,128)(2,1)}, bf16[320,1280]{1,0:T(8,128)(2,1)S(1)}, u32[]{:S(2)}, u32[]{:S(2)}) collective-permute-start(bf16[320,1280]{1,0:T(8,128)(2,1)} %bitcast.22), channel_id=1, source_target_pairs={{0,4},{4,0},{8,12},{12,8},{16,20},{20,16},{24,28},{28,24},{1,5},{5... | collective-permute-start | bytes 2457608 | tf_op jit(solution)/shard_map/ppermute | solution.py:478
  7.8 3.7 %collective-permute-start.1 = (bf16[320,1280]{1,0:T(8,128)(2,1)}, bf16[320,1280]{1,0:T(8,128)(2,1)S(1)}, u32[]{:S(2)}, u32[]{:S(2)}) collective-permute-start(bf16[320,1280]{1,0:T(8,128)(2,1)} %bitcast.35), channel_id=1, source_target_pairs={{0,4},{4,0},{8,12},{12,8},{16,20},{20,16},{24,28},{28,24},{1,5},{5... | collective-permute-start | bytes 2457608 | tf_op jit(solution)/shard_map/ppermute | solution.py:478
  10.1 1.4 collective-permute-start.2
  13.0 7.4 %collective-permute-start.4 = (bf16[256,320]{1,0:T(8,128)(2,1)}, bf16[256,320]{1,0:T(8,128)(2,1)S(1)}, u32[]{:S(2)}, u32[]{:S(2)}) collective-permute-start(bf16[256,320]{1,0:T(8,128)(2,1)} %get-tuple-element.70), channel_id=1, source_target_pairs={{0,8},{4,12},{8,0},{12,4},{16,24},{20,28},{24,16},{28,20},{1,9},{5... | collective-permute-start | bytes 491528 | tf_op jit(solution)/shard_map/ppermute | solution.py:484
  21.1 10.8 %copy-start.26 = (bf16[2,256,320]{2,1,0:T(8,128)(2,1)S(1)}, bf16[2,256,320]{2,1,0:T(8,128)(2,1)}, u32[]{:S(2)}) copy-start(bf16[2,256,320]{2,1,0:T(8,128)(2,1)} %get-tuple-element.83) | copy-start | bytes 983044
  21.3 19.7 %collective-permute-start.5 = (bf16[2,256,320]{2,1,0:T(8,128)(2,1)}, bf16[2,256,320]{2,1,0:T(8,128)(2,1)S(1)}, u32[]{:S(2)}, u32[]{:S(2)}) collective-permute-start(bf16[2,256,320]{2,1,0:T(8,128)(2,1)} %get-tuple-element.76), channel_id=1, source_target_pairs={{8,16},{12,20},{16,8},{20,12},{9,17},{13,21},{17,9},{21,13},{10,18... | collective-permute-start | bytes 983048 | tf_op jit(solution)/shard_map/ppermute | solution.py:490
  31.9 15.4 %collective-permute-start.7 = (bf16[2,256,320]{2,1,0:T(8,128)(2,1)S(1)}, bf16[2,256,320]{2,1,0:T(8,128)(2,1)S(1)}, u32[]{:S(2)}, u32[]{:S(2)}) collective-permute-start(bf16[2,256,320]{2,1,0:T(8,128)(2,1)S(1)} %copy-done.26), channel_id=1, source_target_pairs={{0,24},{4,28},{24,0},{28,4},{1,25},{5,29},{25,1},{29,5},{2,26},{6,... | collective-permute-start | bytes 983048 | tf_op jit(solution)/shard_map/ppermute | solution.py:490
  47.2 6.1 %collective-permute-start.6 = (bf16[256,320]{1,0:T(8,128)(2,1)}, bf16[256,320]{1,0:T(8,128)(2,1)S(1)}, u32[]{:S(2)}, u32[]{:S(2)}) collective-permute-start(bf16[256,320]{1,0:T(8,128)(2,1)} %get-tuple-element.82), channel_id=1, source_target_pairs={{0,8},{4,12},{8,0},{12,4},{16,24},{20,28},{24,16},{28,20},{1,9},{5... | collective-permute-start | bytes 491528 | tf_op jit(solution)/shard_map/ppermute | solution.py:484
  47.3 6.1 %copy-start.9 = (bf16[2,256,320]{2,1,0:T(8,128)(2,1)}, bf16[2,256,320]{2,1,0:T(8,128)(2,1)S(1)}, u32[]{:S(2)}) copy-start(bf16[2,256,320]{2,1,0:T(8,128)(2,1)S(1)} %collective-permute-done.7.refs_1_) | copy-start | bytes 983044
  54.7 16.2 %copy-start.8 = (bf16[256,320]{1,0:T(8,128)(2,1)S(1)}, bf16[256,320]{1,0:T(8,128)(2,1)}, u32[]{:S(2)}) copy-start(bf16[256,320]{1,0:T(8,128)(2,1)} %get-tuple-element.99) | copy-start | bytes 491524
  55.2 1.4 collective-permute-start.9
  57.6 18.5 %collective-permute-start.8 = (bf16[256,320]{1,0:T(8,128)(2,1)S(1)}, bf16[256,320]{1,0:T(8,128)(2,1)S(1)}, u32[]{:S(2)}, u32[]{:S(2)}) collective-permute-start(bf16[256,320]{1,0:T(8,128)(2,1)S(1)} %copy-done.27), channel_id=1, source_target_pairs={{0,8},{4,12},{8,0},{12,4},{16,24},{20,28},{24,16},{28,20},{1,9},{5... | collective-permute-start | bytes 491528 | tf_op jit(solution)/shard_map/ppermute | solution.py:484
  70.9 5.2 %collective-permute-start.10 = (bf16[256,320]{1,0:T(8,128)(2,1)S(1)}, bf16[256,320]{1,0:T(8,128)(2,1)S(1)}, u32[]{:S(2)}, u32[]{:S(2)}) collective-permute-start(bf16[256,320]{1,0:T(8,128)(2,1)S(1)} %copy-done.8), channel_id=1, source_target_pairs={{0,4},{4,0},{8,12},{12,8},{16,20},{20,16},{24,28},{28,24},{1,5},{5... | collective-permute-start | bytes 491528 | tf_op jit(solution)/shard_map/ppermute | solution.py:478
  70.9 11.2 %collective-permute-start.11 = (bf16[256,320]{1,0:T(8,128)(2,1)}, bf16[256,320]{1,0:T(8,128)(2,1)S(1)}, u32[]{:S(2)}, u32[]{:S(2)}) collective-permute-start(bf16[256,320]{1,0:T(8,128)(2,1)} %get-tuple-element.104), channel_id=1, source_target_pairs={{24,8},{28,12},{8,24},{12,28},{25,9},{29,13},{9,25},{13,29},{26,10... | collective-permute-start | bytes 491528 | tf_op jit(solution)/shard_map/ppermute | solution.py:490
  71.6 10.6 %collective-permute-start.12 = (bf16[256,320]{1,0:T(8,128)(2,1)}, bf16[256,320]{1,0:T(8,128)(2,1)S(1)}, u32[]{:S(2)}, u32[]{:S(2)}) collective-permute-start(bf16[256,320]{1,0:T(8,128)(2,1)} %get-tuple-element.97), channel_id=1, source_target_pairs={{24,0},{28,4},{0,24},{4,28},{25,1},{29,5},{1,25},{5,29},{26,2},{30... | collective-permute-start | bytes 491528 | tf_op jit(solution)/shard_map/ppermute | solution.py:490
  82.1 13.7 %copy-start.25 = (bf16[256,320]{1,0:T(8,128)(2,1)}, bf16[256,320]{1,0:T(8,128)(2,1)S(1)}, u32[]{:S(2)}) copy-start(bf16[256,320]{1,0:T(8,128)(2,1)S(1)} %collective-permute-done.11.refs_5_) | copy-start | bytes 491524
  82.1 14.7 %copy-start.23 = (bf16[256,320]{1,0:T(8,128)(2,1)}, bf16[256,320]{1,0:T(8,128)(2,1)S(1)}, u32[]{:S(2)}) copy-start(bf16[256,320]{1,0:T(8,128)(2,1)S(1)} %collective-permute-done.12.refs_4_) | copy-start | bytes 491524
  82.1 13.6 %collective-permute-start.13 = (bf16[2,256,320]{2,1,0:T(8,128)(2,1)}, bf16[2,256,320]{2,1,0:T(8,128)(2,1)S(1)}, u32[]{:S(2)}, u32[]{:S(2)}) collective-permute-start(bf16[2,256,320]{2,1,0:T(8,128)(2,1)} %get-tuple-element.105), channel_id=1, source_target_pairs={{16,8},{20,12},{8,16},{12,20},{17,9},{21,13},{9,17},{13,21},{18,10... | collective-permute-start | bytes 983048 | tf_op jit(solution)/shard_map/ppermute | solution.py:490
  96.8 5.9 %collective-permute-start.14 = (bf16[256,320]{1,0:T(8,128)(2,1)}, bf16[256,320]{1,0:T(8,128)(2,1)S(1)}, u32[]{:S(2)}, u32[]{:S(2)}) collective-permute-start(bf16[256,320]{1,0:T(8,128)(2,1)} %get-tuple-element.109), channel_id=1, source_target_pairs={{0,8},{4,12},{8,0},{12,4},{16,24},{20,28},{24,16},{28,20},{1,9},{5... | collective-permute-start | bytes 491528 | tf_op jit(solution)/shard_map/ppermute | solution.py:484
  103.6 1.7 collective-permute-start.15
  105.4 6.8 %copy-start.12 = (bf16[512,320]{1,0:T(8,128)(2,1)}, bf16[512,320]{1,0:T(8,128)(2,1)S(1)}, u32[]{:S(2)}) copy-start(bf16[512,320]{1,0:T(8,128)(2,1)S(1)} %constant_dynamic-update-slice_fusion.refs_1_) | copy-start | bytes 983044
  105.4 13.4 %collective-permute-start.16 = (bf16[512,320]{1,0:T(8,128)(2,1)S(1)}, bf16[512,320]{1,0:T(8,128)(2,1)S(1)}, u32[]{:S(2)}, u32[]{:S(2)}) collective-permute-start(bf16[512,320]{1,0:T(8,128)(2,1)S(1)} %constant_dynamic-update-slice_fusion.refs_1_), channel_id=1, source_target_pairs={{0,1},{1,0},{2,3},{3,2},{4,5},{5,4},{6,7},{7,6},{8,9},{9,8},{10,11... | collective-permute-start | bytes 983048 | tf_op jit(solution)/shard_map/ppermute | solution.py:498
  108.9 20.9 %collective-permute-start.18 = (bf16[512,320]{1,0:T(8,128)(2,1)S(1)}, bf16[512,320]{1,0:T(8,128)(2,1)S(1)}, u32[]{:S(2)}, u32[]{:S(2)}) collective-permute-start(bf16[512,320]{1,0:T(8,128)(2,1)S(1)} %constant_dynamic-update-slice_fusion.refs_1_), channel_id=1, source_target_pairs={{0,3},{1,2},{2,1},{3,0},{4,7},{5,6},{6,5},{7,4},{8,11},{9,10},{10,... | collective-permute-start | bytes 983048 | tf_op jit(solution)/shard_map/ppermute | solution.py:498
  111.4 34.5 %collective-permute-start.17 = (bf16[512,320]{1,0:T(8,128)(2,1)S(1)}, bf16[512,320]{1,0:T(8,128)(2,1)S(1)}, u32[]{:S(2)}, u32[]{:S(2)}) collective-permute-start(bf16[512,320]{1,0:T(8,128)(2,1)S(1)} %constant_dynamic-update-slice_fusion.refs_1_), channel_id=1, source_target_pairs={{0,2},{1,3},{2,0},{3,1},{4,6},{5,7},{6,4},{7,5},{8,10},{9,11},{10,... | collective-permute-start | bytes 983048 | tf_op jit(solution)/shard_map/ppermute | solution.py:498
  129.1 8.2 %collective-permute-start.19 = (bf16[320,320]{1,0:T(8,128)(2,1)}, bf16[320,320]{1,0:T(8,128)(2,1)S(1)}, u32[]{:S(2)}, u32[]{:S(2)}) collective-permute-start(bf16[320,320]{1,0:T(8,128)(2,1)} %get-tuple-element.133), channel_id=1, source_target_pairs={{0,4},{4,0},{8,12},{12,8},{16,20},{20,16},{24,28},{28,24},{1,5},{5... | collective-permute-start | bytes 614408 | tf_op jit(solution)/shard_map/ppermute | solution.py:478
  145.9 11.2 %copy-start.16 = (bf16[512,320]{1,0:T(8,128)(2,1)}, bf16[512,320]{1,0:T(8,128)(2,1)S(1)}, u32[]{:S(2)}) copy-start(bf16[512,320]{1,0:T(8,128)(2,1)S(1)} %collective-permute-done.17.refs_1_) | copy-start | bytes 983044
  145.9 19.2 %collective-permute-start.22 = (bf16[320,320]{1,0:T(8,128)(2,1)}, bf16[320,320]{1,0:T(8,128)(2,1)S(1)}, u32[]{:S(2)}, u32[]{:S(2)}) collective-permute-start(bf16[320,320]{1,0:T(8,128)(2,1)} %add_merges.2.refs_0_), channel_id=1, source_target_pairs={{16,19},{17,18},{18,17},{19,16},{20,23},{21,22},{22,21},{23,20},{2... | collective-permute-start | bytes 614408 | tf_op jit(solution)/shard_map/ppermute | solution.py:498
  152.1 20.2 %collective-permute-start.21 = (bf16[320,320]{1,0:T(8,128)(2,1)}, bf16[320,320]{1,0:T(8,128)(2,1)S(1)}, u32[]{:S(2)}, u32[]{:S(2)}) collective-permute-start(bf16[320,320]{1,0:T(8,128)(2,1)} %add_merges.2.refs_0_), channel_id=1, source_target_pairs={{16,18},{17,19},{18,16},{19,17},{20,22},{21,23},{22,20},{23,21},{2... | collective-permute-start | bytes 614408 | tf_op jit(solution)/shard_map/ppermute | solution.py:498
  154.3 18.1 %collective-permute-start.20 = (bf16[320,320]{1,0:T(8,128)(2,1)}, bf16[320,320]{1,0:T(8,128)(2,1)S(1)}, u32[]{:S(2)}, u32[]{:S(2)}) collective-permute-start(bf16[320,320]{1,0:T(8,128)(2,1)} %add_merges.2.refs_0_), channel_id=1, source_target_pairs={{16,17},{17,16},{18,19},{19,18},{20,21},{21,20},{22,23},{23,22},{2... | collective-permute-start | bytes 614408 | tf_op jit(solution)/shard_map/ppermute | solution.py:498
  165.1 7.2 %copy-start.19 = (bf16[320,320]{1,0:T(8,128)(2,1)}, bf16[320,320]{1,0:T(8,128)(2,1)S(1)}, u32[]{:S(2)}) copy-start(bf16[320,320]{1,0:T(8,128)(2,1)S(1)} %collective-permute-done.22.refs_3_) | copy-start | bytes 614404
  (20 other events, 25.0 us)
Sparse Core Ops, SparseCore 0:
  57.7 52.5 all-gather.2
